TPU v7x, 256 devices: a whole 4x4x8 slice. The times are simulated.
256 devices in a mesh: rows: 32 (over y, x, core), feat: 8 (over z).
Axes of the slice: x: 4, y: 4, z: 8, core: 2. Of those that a mesh axis runs over, the one named last changes fastest.
Arguments:
- features: bfloat16 [65536, 768], P('rows', 'feat'), may hold values from -6 to 6
- pair_doc: int32 [768], P('rows'), may hold values from 0 to 127, as said below
- pair_label: int32 [768], P('rows'), may hold values from 0 to 127, as said below
- incidence: bfloat16 [768, 512, 512], P('rows'), may hold values from 0 to 1, as said below
- weight: bfloat16 [768, 768], P('feat'), may hold values from -0.21875 to 0.21875
- cotangent: bfloat16 [65536, 768], P('rows', 'feat'), may hold values from -6 to 6
Outputs:
- activated: bfloat16 [65536, 768], P('rows', 'feat')
- weight_grad: float32 [768, 768], P('feat')
- feature_grad: bfloat16 [65536, 768], P('rows', 'feat')
Inputs may be any that keep to these rules, and one draw needn't show every extreme that they name: `pair_doc`: pair i belongs to rows index i // 24 and its document tile is one of that index's tiles, (i // 24) * 4 to (i // 24 + 1) * 4 - 1. `pair_label`: label block b is owned by rows index b // 4. The 24 pairs of one rows index go to exactly 8 distinct owners, 3 pairs to each. `incidence`: each entry is zero or a positive edge weight.
All inputs are finite; a program needn't handle non-finite values.
Results may differ from a plain program's by a relative error of at most 0.0066.
Values may be sent and summed in bfloat16 or wider, within the bound.
A program may use at most 128 MiB of HBM per device.

v0:
```python
import jax
import jax.numpy as jnp
from jax import lax
from jax.sharding import PartitionSpec as P

LB_DEV = 4
CAPO = 3


message_scale = 0.0625


def slot_ranks(owner_ids):
    pair_count = owner_ids.shape[-1]
    same = owner_ids[..., :, None] == owner_ids[..., None, :]
    earlier = jnp.arange(pair_count)[None, :] < jnp.arange(pair_count)[:, None]
    return jnp.sum(jnp.where(same & earlier, 1, 0), axis=-1).astype(jnp.int32)


def local(features, pair_doc, pair_label, incidence, weight, cotangent):
    tile_rows = incidence.shape[1]
    pair_count = incidence.shape[0]
    slice_width = features.shape[1]
    owner_count = lax.axis_size("rows")
    rows_rank = lax.axis_index("rows")
    doc_tiles = features.shape[0] // tile_rows
    label_rows = cotangent.shape[0]
    local_doc = pair_doc - rows_rank * doc_tiles
    doc_stack = features.reshape(doc_tiles, tile_rows, slice_width)
    pair_docs = jnp.take(doc_stack, local_doc, axis=0)
    products = (
        message_scale
        * jnp.einsum("pdl,pdw->plw", incidence, pair_docs, preferred_element_type=jnp.float32)
    ).astype(jnp.bfloat16)
    every_label = lax.all_gather(pair_label, "rows", axis=0, tiled=True).reshape(
        owner_count, pair_count
    )
    every_owner = every_label // LB_DEV
    every_rank = slot_ranks(every_owner)
    my_owner = pair_label // LB_DEV
    my_slot = my_owner * CAPO + slot_ranks(my_owner)
    outgoing = (
        jnp.zeros((owner_count * CAPO, tile_rows, slice_width), jnp.bfloat16)
        .at[my_slot]
        .set(products)
    )
    incoming = lax.all_to_all(
        outgoing.reshape(owner_count, CAPO * tile_rows, slice_width),
        "rows",
        split_axis=0,
        concat_axis=0,
        tiled=True,
    )
    match = (every_owner == rows_rank)[:, :, None] & (
        every_rank[:, :, None] == jnp.arange(CAPO)[None, None, :]
    )
    filled = jnp.any(match, axis=1)
    slot_block = jnp.sum(
        jnp.where(match, (every_label - rows_rank * LB_DEV)[:, :, None], 0), axis=1
    )
    select = filled[None, :, :] & (slot_block[None, :, :] == jnp.arange(LB_DEV)[:, None, None])
    select = select.astype(jnp.bfloat16).reshape(LB_DEV, owner_count * CAPO)
    summed = jnp.dot(
        select,
        incoming.reshape(owner_count * CAPO, tile_rows * slice_width),
        preferred_element_type=jnp.float32,
    )
    messages = summed.reshape(label_rows, slice_width).astype(jnp.bfloat16)
    weight_full = lax.all_gather(weight, "feat", axis=0, tiled=True)
    feat_rank = lax.axis_index("feat")
    columns = lax.dynamic_slice_in_dim(weight_full, feat_rank * slice_width, slice_width, 1)
    weight_part = columns
    mixed = jnp.dot(
        lax.all_gather(messages, "feat", axis=1, tiled=True),
        weight_part,
        preferred_element_type=jnp.float32,
    )
    gate_value = jax.nn.sigmoid(mixed)
    activated = (mixed * gate_value).astype(jnp.bfloat16)
    slope = gate_value * (1.0 + mixed * (1.0 - gate_value))
    grad_mixed = (cotangent.astype(jnp.float32) * slope).astype(jnp.bfloat16)
    grad_full = lax.all_gather(grad_mixed, "feat", axis=1, tiled=True)
    weight_part = lax.dot_general(
        messages, grad_full, (((0,), (0,)), ((), ())), preferred_element_type=jnp.float32
    )
    weight_grad = lax.psum(weight_part, "rows")
    grad_messages = lax.dot_general(
        grad_full, weight, (((1,), (1,)), ((), ())), preferred_element_type=jnp.float32
    ).astype(jnp.bfloat16)
    grad_blocks = grad_messages.reshape(LB_DEV, tile_rows, slice_width)
    every_block = lax.all_gather(grad_blocks, "rows", axis=0, tiled=True)
    pair_grads = jnp.take(every_block, pair_label, axis=0)
    terms = jnp.einsum("pdl,plw->pdw", incidence, pair_grads, preferred_element_type=jnp.float32)
    doc_onehot = (local_doc[None, :] == jnp.arange(doc_tiles)[:, None]).astype(jnp.float32)
    doc_totals = jnp.einsum("tp,pdw->tdw", doc_onehot, terms, precision=lax.Precision.HIGHEST)
    feature_grad = doc_totals.reshape(doc_tiles * tile_rows, slice_width).astype(jnp.bfloat16)
    return (activated, weight_grad, feature_grad)


def solution(mesh):
    return jax.shard_map(
        local,
        mesh=mesh,
        in_specs=(
            P("rows", "feat"),
            P("rows"),
            P("rows"),
            P("rows", None, None),
            P("feat", None),
            P("rows", "feat"),
        ),
        out_specs=(P("rows", "feat"), P("feat", None), P("rows", "feat")),
        check_vma=False,
    )
```

profile of v0, /device:TPU:1, one launch (start us, length us, event | category | flops | bytes accessed | tf_op | source)
XLA Modules:
  0.0 532.4 jit_solution(2975689789123172695)
XLA Ops:
  7.2 0.7 compare_and_fusion.1
  7.8 1.0 copy.61
  8.9 0.7 compare_select_fusion.2
  9.7 0.7 gather_fusion
  10.4 8.1 %fusion.2 = bf16[24,512,96]{1,2,0:T(8,128)(2,1)} fusion(bf16[24,512,512]{2,1,0:T(8,128)(2,1)} %param.9, bf16[24,512,96]{1,2,0:T(8,128)(2,1)S(1)} %gather_fusion, pred[24]{0:T(512)(128)(4,1)S(1)} %get-tuple-element.5), kind=kOutput, calls=%fused_computation.7 | convolution fusion | flops 1211498496 | bytes 17301528 | tf_op jit(solution)/shard_map/pdl,pdw->plw/dot_general | solution.py:33
  18.6 4.8 broadcast_in_dim.78
  23.4 7.2 %scatter_fusion = bf16[96,512,96]{1,2,0:T(8,128)(2,1)} fusion(bf16[96,512,96]{1,2,0:T(8,128)(2,1)} %broadcast_in_dim.78, s32[24]{0:T(128)S(1)} %compare_select_fusion.1, bf16[24,512,96]{1,2,0:T(8,128)(2,1)S(1)} %copy-done), kind=kCustom, calls=%fused_computation.2 | custom fusion | bytes 7077984 | tf_op jit(solution)/shard_map/scatter | solution.py:45
  30.6 12.7 %copy.45 = bf16[96,512,96]{1,0,2:T(8,128)(2,1)} copy(bf16[96,512,96]{1,2,0:T(8,128)(2,1)} %scatter_fusion) | data formatting | bytes 18874368 | tf_op jit(solution)/shard_map/scatter | solution.py:45
  43.3 15.0 %reshape.131 = bf16[32,1536,96]{1,0,2:T(8,128)(2,1)} reshape(bf16[96,512,96]{1,0,2:T(8,128)(2,1)} %copy.45) | data formatting | bytes 18874368 | tf_op jit(solution)/shard_map/reshape | solution.py:48
  58.2 12.5 %copy.46 = bf16[32,1536,96]{1,2,0:T(8,128)(2,1)} copy(bf16[32,1536,96]{1,0,2:T(8,128)(2,1)} %reshape.131) | data formatting | bytes 18874368 | tf_op jit(solution)/shard_map/reshape | solution.py:48
  70.8 8.8 %all-to-all-start = ((bf16[32,1536,96]{1,2,0:T(8,128)(2,1)}), bf16[32,1536,96]{1,2,0:T(8,128)(2,1)}, u32[]{:S(2)}, u32[]{:S(2)}) async-start(bf16[32,1536,96]{1,2,0:T(8,128)(2,1)} %copy.46), calls=%async_computation | async-start | bytes 18874368 | tf_op jit(solution)/shard_map/all_to_all | solution.py:47
  79.6 0.7 all-gather.7.cloned.1.call-update
  80.3 0.6 dynamic-slice
  81.9 120.1 %all-reduce = s32[768]{0:T(1024)S(1)} all-reduce(s32[768]{0:T(1024)S(1)} %dynamic-update-slice), channel_id=1, replica_groups=mesh['rows'=32,'feat'=8] {'rows'}, use_global_device_ids=true, to_apply=%add | all-reduce | flops 768 | bytes 6144
  202.9 14.6 %copy.47 = bf16[32,1536,96]{2,1,0:T(8,128)(2,1)} copy(bf16[32,1536,96]{1,2,0:T(8,128)(2,1)} %all-to-all-done) | data formatting | bytes 18874368 | tf_op jit(solution)/shard_map/all_to_all | solution.py:47
  217.5 20.2 %reshape.132 = bf16[96,49152]{1,0:T(8,128)(2,1)} reshape(bf16[32,1536,96]{2,1,0:T(8,128)(2,1)} %copy.47) | data formatting | bytes 18874368 | tf_op jit(solution)/shard_map/reshape | solution.py:65
  237.7 5.1 convolution_convert_fusion
  242.8 0.4 convert_element_type.35
  243.2 1.0 copy.48
  244.3 47.9 %all-gather.5.cloned.1.call-done = bf16[2048,768]{0,1:T(8,128)(2,1)} async-done(((bf16[2048,96]{0,1:T(8,128)(2,1)}), bf16[2048,768]{0,1:T(8,128)(2,1)}) %all-gather.5.cloned.1.call-update) | async-done | bytes 3145744 | tf_op jit(solution)/shard_map/all_gather | solution.py:74
  292.2 3.8 multiply_convert_fusion.1
  296.1 43.7 %all-gather.9.cloned.1.call-done = bf16[2048,768]{0,1:T(8,128)(2,1)} async-done(((bf16[2048,96]{0,1:T(8,128)(2,1)}), bf16[2048,768]{0,1:T(8,128)(2,1)}) %all-gather.9.cloned.1.call-update) | async-done | bytes 3145744 | tf_op jit(solution)/shard_map/all_gather | solution.py:82
  339.8 2.7 convolution_convert_fusion.1
  342.5 0.8 copy.60
  343.6 2.9 fusion.35
  346.5 64.1 %all-gather.11.cloned.1.call-done = bf16[128,512,96]{1,2,0:T(8,128)(2,1)} async-done(((bf16[4,512,96]{1,2,0:T(8,128)(2,1)}), bf16[128,512,96]{1,2,0:T(8,128)(2,1)}) %all-gather.11.cloned.1.call-update) | async-done | bytes 12582928 | tf_op jit(solution)/shard_map/all_gather | solution.py:91
  410.6 6.8 %gather_fusion.1 = bf16[24,512,96]{1,2,0:T(8,128)(2,1)} fusion(bf16[128,512,96]{1,2,0:T(8,128)(2,1)} %all-gather.11.cloned.1.call-done, s32[1024]{0:T(1024)S(1)} %pad_clamp_fusion), kind=kCustom, calls=%fused_computation.1 | custom fusion | bytes 4718688 | tf_op jit(solution)/shard_map/jit(_take)/gather | solution.py:92
  417.4 9.2 %fusion.9 = f32[24,512,96]{1,2,0:T(8,128)S(1)} fusion(bf16[24,512,512]{2,1,0:T(8,128)(2,1)} %param.9, bf16[24,512,96]{1,2,0:T(8,128)(2,1)} %gather_fusion.1, pred[24]{0:T(512)(128)(4,1)S(1)} %compare_and_fusion), kind=kOutput, calls=%fused_computation.15 | convolution fusion | flops 1209139200 | bytes 19660824 | tf_op jit(solution)/shard_map/pdl,plw->pdw/dot_general | solution.py:93
  426.6 4.3 fusion.14
  430.9 0.8 copy.53
  431.7 92.4 %all-reduce.3.cloned.1.call-done = f32[96,768]{1,0:T(8,128)} async-done(((f32[96,768]{1,0:T(8,128)}), f32[96,768]{1,0:T(8,128)}) %all-reduce.3.cloned.1.call-update) | async-done | bytes 294928 | tf_op jit(solution)/shard_map/psum | solution.py:86
  524.2 1.7 copy.65
  (46 shorter events, 1.9 us)
Async XLA Ops:
  18.6 4.8 copy-start
  70.8 9.6 %copy-start.6 = (u32[256]{0:T(256)S(1)}, u32[256]{0:T(256)}, u32[]{:S(2)}) copy-start(u32[256]{0:T(256)} %constant.84) | copy-start | bytes 3076
  70.8 10.8 %copy-start.5 = (s32[24]{0:T(128)S(1)}, s32[24]{0:T(128)}, u32[]{:S(2)}) copy-start(s32[24]{0:T(128)} %param.8) | copy-start | bytes 292
  70.8 132.1 %all-to-all-start = ((bf16[32,1536,96]{1,2,0:T(8,128)(2,1)}), bf16[32,1536,96]{1,2,0:T(8,128)(2,1)}, u32[]{:S(2)}, u32[]{:S(2)}) async-start(bf16[32,1536,96]{1,2,0:T(8,128)(2,1)} %copy.46), calls=%async_computation | async-start | bytes 18874368 | tf_op jit(solution)/shard_map/all_to_all | solution.py:47
  79.5 164.7 %all-gather.7.cloned.1.call-start = ((), (), s32[]{:S(2)}) async-start(), calls=%async_computation.2 | async-start | bytes 1327104 | tf_op jit(solution)/shard_map/all_gather | solution.py:69
  80.3 211.9 %all-gather.5.cloned.1.call-start = ((), (), s32[]{:S(2)}) async-start(), calls=%async_computation.1 | async-start | bytes 3538944 | tf_op jit(solution)/shard_map/all_gather | solution.py:74
  237.7 54.5 %copy-start.4 = (bf16[2048,96]{0,1:T(8,128)(2,1)S(1)}, bf16[2048,96]{0,1:T(8,128)(2,1)}, u32[]{:S(2)}) copy-start(bf16[2048,96]{0,1:T(8,128)(2,1)} %param.11) | copy-start | bytes 1179652
  243.2 52.8 %copy-start.2 = (bf16[2048,96]{1,0:T(8,128)(2,1)}, bf16[2048,96]{1,0:T(8,128)(2,1)S(1)}, u32[]{:S(2)}) copy-start(bf16[2048,96]{1,0:T(8,128)(2,1)S(1)} %convert_element_type.35) | copy-start | bytes 1179652
  244.2 95.6 %all-gather.9.cloned.1.call-start = ((), (), s32[]{:S(2)}) async-start(), calls=%async_computation.3 | async-start | bytes 3538944 | tf_op jit(solution)/shard_map/all_gather | solution.py:82
  244.3 95.5 %copy-start.3 = (bf16[96,768]{1,0:T(8,128)(2,1)S(1)}, bf16[96,768]{1,0:T(8,128)(2,1)}, u32[]{:S(2)}) copy-start(bf16[96,768]{1,0:T(8,128)(2,1)} %param.10) | copy-start | bytes 442372
  296.0 114.6 %all-gather.11.cloned.1.call-start = ((), (), s32[]{:S(2)}) async-start(), calls=%async_computation.5 | async-start | bytes 12976128 | tf_op jit(solution)/shard_map/all_gather | solution.py:91
  339.8 3.8 copy-start.1
  343.3 180.9 %all-reduce.3.cloned.1.call-start = ((), (), s32[]{:S(2)}) async-start(), calls=%async_computation.4 | async-start | bytes 589824 | tf_op jit(solution)/shard_map/psum | solution.py:86
Sparse Core Ops, SparseCore 0:
  82.2 38.0 all-gather.6
  244.3 47.8 all-gather.4
  296.1 43.6 all-gather.8
  343.4 67.1 all-gather.10
  414.3 109.7 all-reduce.2
where the time goes:
time: 534 us; the launch traced here: 532 us
  waiting for transfers between devices  249 us (47%)
  blocking collectives  120 us (22%)
  local copies, waits for them, and re-layouts  102 us (19%)
  matrix products  36 us (7%)
  between operations  14.6 us (3%)
  starting transfers between devices  9.24 us (2%)
    unnamed x1, blocking collectives  120 us
    psum x1, waiting for transfers between devices, local(): weight_grad = lax.psum(weight_part, 'rows')  92.4 us
    all_gather x1, waiting for transfers between devices, local(): every_block = lax.all_gather(grad_blocks, 'rows', axis=0, tiled=True)  64.1 us
    all_gather x1, waiting for transfers between devices, local(): lax.all_gather(messages, 'feat', axis=1, tiled=True)  47.9 us
    all_gather x1, waiting for transfers between devices, local(): grad_full = lax.all_gather(grad_mixed, 'feat', axis=1, tiled=True)  43.7 us
    reshape x2, local copies, waits for them, and re-layouts, local(): outgoing.reshape(owner_count, CAPO * tile_rows, slice_width)  27.5 us
    reshape x1, local copies, waits for them, and re-layouts, local(): incoming.reshape(owner_count * CAPO, tile_rows * slice_width)  20.2 us
    scatter x2, local copies, waits for them, and re-layouts, local(): outgoing = jnp.zeros((owner_count * CAPO, tile_rows, slice_width), jnp.bf...  19.9 us
  transfers between devices with their start and end apart: 6, of which 4 were waited for; matrix products, arithmetic and copies ran while one was open for 13% of the time, Pallas kernels for 0%

commit v1 on v0

v1 whole, which is shorter than its diff:
```python
import functools

import jax
import jax.numpy as jnp
from jax import lax
from jax.experimental import pallas as pl
from jax.experimental.pallas import tpu as pltpu
from jax.sharding import PartitionSpec as P

MESH = pl.DeviceIdType.MESH
message_scale = 0.0625

SIDE = 4
FEAT = 8
LB = 4
CAP = 3
TILE = 512
PAIRS = 24
W = 96
D = 768
GROUP = 4
BLOCKS = 128
CHUNK = 256
VMEM_LIMIT = 60 * 1024 * 1024

f32, bf16 = jnp.float32, jnp.bfloat16


def forward_kernel(doc_ref, label_ref, feat_ref, inc_ref, msg_ref, table_ref):
    step = pl.program_id(0)
    rows = lax.axis_index("rows")

    @pl.when(step == 0)
    def _():
        msg_ref[PAIRS] = jnp.zeros((W, TILE), bf16)

        def clear(i, carry):
            table_ref[i] = PAIRS
            return carry

        lax.fori_loop(0, BLOCKS * CAP, clear, 0)

        def place(p, carry):
            base = label_ref[p] * CAP
            first = table_ref[base] == PAIRS
            second = table_ref[base + 1] == PAIRS
            spot = jnp.where(first, 0, jnp.where(second, 1, 2))
            table_ref[base + spot] = p
            return carry

        lax.fori_loop(0, PAIRS, place, 0)

    for k in range(GROUP):
        p = step * GROUP + k
        tile = doc_ref[p] - rows * (feat_ref.shape[1] // TILE)
        piece = feat_ref[:, pl.ds(pl.multiple_of(tile * TILE, TILE), TILE)]
        product = jnp.dot(piece, inc_ref[k], preferred_element_type=f32)
        msg_ref[p] = (message_scale * product).astype(bf16)


def forward_pairs(doc, label, feat, inc):
    return pl.pallas_call(
        forward_kernel,
        grid_spec=pltpu.PrefetchScalarGridSpec(
            num_scalar_prefetch=2,
            grid=(PAIRS // GROUP,),
            in_specs=[
                pl.BlockSpec((W, feat.shape[1]), lambda i, d, l: (0, 0)),
                pl.BlockSpec((GROUP, TILE, TILE), lambda i, d, l: (i, 0, 0)),
            ],
            out_specs=[
                pl.BlockSpec((PAIRS + 1, W, TILE), lambda i, d, l: (0, 0, 0)),
                pl.BlockSpec(memory_space=pltpu.SMEM),
            ],
        ),
        out_shape=[
            jax.ShapeDtypeStruct((PAIRS + 1, W, TILE), bf16),
            jax.ShapeDtypeStruct((BLOCKS * CAP,), jnp.int32),
        ],
        compiler_params=pltpu.CompilerParams(vmem_limit_bytes=VMEM_LIMIT),
    )(doc, label, feat, inc)


def backward_kernel(doc_ref, label_ref, *refs):
    grads, inc_ref, out_ref, acc = refs[:GROUP], refs[GROUP], refs[GROUP + 1], refs[GROUP + 2]
    step = pl.program_id(0)
    rows = lax.axis_index("rows")
    tiles = acc.shape[0]

    @pl.when(step == 0)
    def _():
        acc[...] = jnp.zeros_like(acc)

    for k in range(GROUP):
        tile = doc_ref[step * GROUP + k] - rows * tiles
        acc[tile] += lax.dot_general(
            grads[k][0], inc_ref[k], (((1,), (1,)), ((), ())), preferred_element_type=f32
        )

    @pl.when(step == PAIRS // GROUP - 1)
    def _():
        for t in range(tiles):
            out_ref[:, t * TILE : (t + 1) * TILE] = acc[t].astype(bf16)


def backward_pairs(doc, label, grads, inc, width):
    def pick(k):
        return lambda i, d, l: (l[i * GROUP + k], 0, 0)

    return pl.pallas_call(
        backward_kernel,
        grid_spec=pltpu.PrefetchScalarGridSpec(
            num_scalar_prefetch=2,
            grid=(PAIRS // GROUP,),
            in_specs=[pl.BlockSpec((1, W, TILE), pick(k)) for k in range(GROUP)]
            + [pl.BlockSpec((GROUP, TILE, TILE), lambda i, d, l: (i, 0, 0))],
            out_specs=pl.BlockSpec((W, width), lambda i, d, l: (0, 0)),
            scratch_shapes=[pltpu.VMEM((width // TILE, W, TILE), f32)],
        ),
        out_shape=jax.ShapeDtypeStruct((W, width), bf16),
        compiler_params=pltpu.CompilerParams(vmem_limit_bytes=VMEM_LIMIT),
    )(doc, label, *([grads] * GROUP), inc)


def wait(ref, sem):
    pltpu.make_async_copy(ref, ref, sem).wait()


def offset(i):
    return 2 - i + 3 * (i // 2) - 2 * (i // 3)


def exchange_kernel(
    table, msg, weight, cot,
    act_out, wg_out, grads,
    sib_send, sib_recv, s1_send, s1_recv, s2_send, s2_recv, t1_send, t1_recv, t2_send, t2_recv,
    summed, xin, wfull, cot_in, act_buf, gm_buf, gmt_buf,
    wgp, wgc_recv, wgz_send, wgz_recv, wx_send, wx_recv, wy_send, wy_recv, wf_send, wf_recv, wg_half,
    sib_ss, sib_rs, s1_ss, s1_rs, s2_ss, s2_rs, t_ss, t1_rs, t2_rs,
    z_ss, x_rs, w_rs, cot_rs, act_rs, gz_rs, local_sem,
    ag_ss, p1_rs, p2_rs, q1_rs, q2_rs, pair_rs,
    wg_ss, wgc_rs, wgz_rs, wx_rs, wy_rs, wf_rs, wl_rs,
):
    r, z = lax.axis_index("rows"), lax.axis_index("feat")
    core, x, y = lax.rem(r, 2), lax.rem(r // 2, SIDE), r // (2 * SIDE)

    def around(value, step):
        return lax.rem(value + step + 2 * SIDE, SIDE)

    def row_of(yy, xx, cc):
        return (yy * SIDE + xx) * 2 + cc

    place = ((x, y), (y, x))

    def owner(h, u, v, cc):
        return row_of(v, u, cc) if h == 0 else row_of(u, v, cc)

    def near(h, du, dv):
        u, v = place[h]
        return {"rows": owner(h, around(u, du), around(v, dv), core), "feat": z}

    sibling = {"rows": row_of(y, x, 1 - core), "feat": z}

    def along_z(d):
        return lax.rem(z + d, FEAT)

    def send(src, dst, ss, rs, target):
        pltpu.make_async_remote_copy(
            src_ref=src, dst_ref=dst, send_sem=ss, recv_sem=rs, device_id=target, device_id_type=MESH
        ).start()

    barrier = pltpu.get_barrier_semaphore()
    partners = [sibling]
    for d in range(1, SIDE):
        partners += [near(0, d, 0), near(1, d, 0)]
    for d in range(1, FEAT):
        partners.append({"rows": r, "feat": along_z(d)})
    for target in partners:
        pl.semaphore_signal(barrier, inc=1, device_id=target, device_id_type=MESH)
    pl.semaphore_wait(barrier, len(partners))

    def block_id(h, u, v, j, cc):
        return owner(h, u, v, cc) * LB + 2 * h + j

    def own_part(block):
        base = block * CAP
        total = msg[table[base]].astype(f32)
        for k in range(1, CAP):
            total = total + msg[table[base + k]].astype(f32)
        return total

    def slot(g, i, h, j):
        return ((g * SIDE + i) * 2 + h) * 2 + j

    def pair_part(g, du, i):
        for h in range(2):
            u, v = place[h]
            for j in range(2):
                k = slot(g, i, h, j)
                block = block_id(h, around(u, du), around(v, offset(i)), j, 1 - core)
                sib_send[k] = own_part(block).astype(bf16)
                send(sib_send.at[k], sib_recv.at[k], sib_ss, sib_rs.at[k], sibling)

    def merged(g, du, i, h, j):
        u, v = place[h]
        k = slot(g, i, h, j)
        part = own_part(block_id(h, around(u, du), around(v, offset(i)), j, core))
        wait(sib_recv.at[k], sib_rs.at[k])
        return part + sib_recv[k].astype(f32)

    def loop(n, body):
        lax.fori_loop(0, n, lambda i, c: (body(i), c)[1], 0)

    loop(SIDE, lambda i: pair_part(0, 2, i))

    def first(i):
        for h in range(2):
            for j in range(2):
                k = slot(0, i, h, j)
                s1_send[k] = merged(0, 2, i, h, j).astype(bf16)
                send(s1_send.at[k], s1_recv.at[k], s1_ss, s1_rs.at[k], near(h, 1 - 2 * j, 0))
        pair_part(1, 1, i)
        pair_part(2, -1, i)

    loop(SIDE, first)

    def spread(d):
        zz = along_z(d)
        target = {"rows": r, "feat": zz}
        mine = pl.ds(pl.multiple_of(z * W, W), W)
        send(weight, wfull.at[mine, :], z_ss.at[0], w_rs.at[z], target)
        lanes = pl.ds(pl.multiple_of(zz * CHUNK, CHUNK), CHUNK)
        send(cot.at[:, lanes], cot_in.at[mine, :], z_ss.at[1], cot_rs.at[z], target)

    lax.fori_loop(1, FEAT, lambda d, c: (spread(d), c)[1], 0)
    own_rows = pl.ds(pl.multiple_of(z * W, W), W)
    own_lanes = pl.ds(pl.multiple_of(z * CHUNK, CHUNK), CHUNK)
    wfull[own_rows, :] = weight[...]
    cot_in[own_rows, :] = cot[:, own_lanes]

    def second(i):
        for h in range(2):
            for way in range(2):
                du = 1 - 2 * way
                for j in (1 - way, way):
                    k = slot(way, i, h, j)
                    total = merged(1 + way, du, i, h, j)
                    if j == way:
                        q = slot(0, i, h, j)
                        wait(s1_recv.at[q], s1_rs.at[q])
                        total = total + s1_recv[q].astype(f32)
                    s2_send[k] = total.astype(bf16)
                    send(s2_send.at[k], s2_recv.at[k], s2_ss, s2_rs.at[k], near(h, du, 0))
        pair_part(3, 0, i)

    loop(SIDE, second)

    def column(i, h, j):
        total = merged(3, 0, i, h, j)
        for way in range(2):
            k = slot(way, i, h, j)
            wait(s2_recv.at[k], s2_rs.at[k])
            total = total + s2_recv[k].astype(f32)
        return total

    for h in range(2):
        for j in range(2):
            k = 2 * h + j
            t1_send[k] = column(0, h, j).astype(bf16)
            send(t1_send.at[k], t1_recv.at[k], t_ss.at[0], t1_rs.at[k], near(h, 0, 1 - 2 * j))
    for way in range(2):
        for h in range(2):
            for j in (1 - way, way):
                k = (way * 2 + h) * 2 + j
                total = column(1 + way, h, j)
                if j == way:
                    q = 2 * h + j
                    wait(t1_recv.at[q], t1_rs.at[q])
                    total = total + t1_recv[q].astype(f32)
                t2_send[k] = total.astype(bf16)
                send(t2_send.at[k], t2_recv.at[k], t_ss.at[1], t2_rs.at[k], near(h, 0, 1 - 2 * way))
    for h in range(2):
        for j in range(2):
            total = column(3, h, j)
            for way in range(2):
                k = (way * 2 + h) * 2 + j
                wait(t2_recv.at[k], t2_rs.at[k])
                total = total + t2_recv[k].astype(f32)
            summed[2 * h + j] = total.astype(bf16)

    def half_lanes(zz):
        return pl.ds(pl.multiple_of(lax.rem(zz, 2) * CHUNK, CHUNK), CHUNK)

    def gather_features(d):
        zz = along_z(d)
        send(summed.at[zz // 2, :, half_lanes(zz)], xin.at[own_rows, :], z_ss.at[2], x_rs.at[z],
             {"rows": r, "feat": zz})

    lax.fori_loop(1, FEAT, lambda d, c: (gather_features(d), c)[1], 0)
    xin[own_rows, :] = summed[z // 2, :, half_lanes(z)]

    def arrive(ref, sems):
        def one(d):
            zz = along_z(d)
            wait(ref.at[pl.ds(pl.multiple_of(zz * W, W), W), :], sems.at[zz])

        lax.fori_loop(1, FEAT, lambda d, c: (one(d), c)[1], 0)

    arrive(wfull, w_rs)
    arrive(cot_in, cot_rs)
    arrive(xin, x_rs)

    def mix(o):
        rows = pl.ds(pl.multiple_of(o * CHUNK, CHUNK), CHUNK)
        mixed = lax.dot_general(
            wfull[:, rows], xin[...], (((0,), (0,)), ((), ())), preferred_element_type=f32
        )
        gate = jax.nn.sigmoid(mixed)
        act_buf[rows, :] = (mixed * gate).astype(bf16)
        slope = gate * (1.0 + mixed * (1.0 - gate))
        gm_buf[rows, :] = (cot_in[rows, :].astype(f32) * slope).astype(bf16)

    loop(D // CHUNK, mix)

    def unmix(o):
        rows = pl.ds(pl.multiple_of(o * CHUNK, CHUNK), CHUNK)
        gmt_buf[rows, :] = jnp.dot(wfull[rows, :], gm_buf[...], preferred_element_type=f32).astype(bf16)

    loop(D // CHUNK, unmix)

    def give_back(d):
        zz = along_z(d)
        rows = pl.ds(pl.multiple_of(zz * W, W), W)
        target = {"rows": r, "feat": zz}
        send(gmt_buf.at[rows, :], grads.at[r * LB + z // 2, :, half_lanes(z)], z_ss.at[3], gz_rs.at[z], target)

    def give_act(d):
        zz = along_z(d)
        rows = pl.ds(pl.multiple_of(zz * W, W), W)
        target = {"rows": r, "feat": zz}
        send(act_buf.at[rows, :], act_out.at[:, own_lanes], z_ss.at[4], act_rs.at[z], target)

    lax.fori_loop(1, FEAT, lambda d, c: (give_back(d), c)[1], 0)
    own_grad = pltpu.make_async_copy(
        gmt_buf.at[own_rows, :], grads.at[r * LB + z // 2, :, half_lanes(z)], local_sem.at[0]
    )
    own_grad.start()
    lax.fori_loop(1, FEAT, lambda d, c: (give_act(d), c)[1], 0)
    own_act = pltpu.make_async_copy(act_buf.at[own_rows, :], act_out.at[:, own_lanes], local_sem.at[1])
    own_act.start()

    HALF = W // 2

    def weight_term(s):
        rows = pl.ds(pl.multiple_of(s * CHUNK, CHUNK), CHUNK)
        wgp[rows, :] = lax.dot_general(
            xin[rows, :], gm_buf[...], (((1,), (1,)), ((), ())), preferred_element_type=f32
        )

    loop(D // CHUNK, weight_term)

    def slab(s, cc):
        return pl.ds(pl.multiple_of(s * W + cc * HALF, HALF), HALF)

    def to_sibling(s):
        send(wgp.at[slab(s, 1 - core), :], wgc_recv.at[s], wg_ss.at[0], wgc_rs.at[s], sibling)

    loop(FEAT, to_sibling)

    def to_z(d):
        zz = along_z(d)
        wait(wgc_recv.at[zz], wgc_rs.at[zz])
        wgz_send[zz] = (wgp[slab(zz, core), :] + wgc_recv[zz]).astype(bf16)
        send(wgz_send.at[zz], wgz_recv.at[z], wg_ss.at[1], wgz_rs.at[z], {"rows": r, "feat": zz})

    lax.fori_loop(1, FEAT, lambda d, c: (to_z(d), c)[1], 0)
    wait(wgc_recv.at[z], wgc_rs.at[z])

    own_grad.wait()

    def grads_in(d):
        zz = along_z(d)
        wait(grads.at[r * LB + zz // 2, :, half_lanes(zz)], gz_rs.at[zz])

    lax.fori_loop(1, FEAT, lambda d, c: (grads_in(d), c)[1], 0)

    def share(block):
        send(grads.at[block], grads.at[block], ag_ss, pair_rs, sibling)

    def pass_on(block, rs, target):
        send(grads.at[block], grads.at[block], ag_ss, rs, target)

    def at(h, du, dv, j):
        u, v = place[h]
        return block_id(h, around(u, du), around(v, dv), j, core)

    def four(way, h, j):
        return (way * 2 + h) * 2 + j

    for way in range(2):
        for h in range(2):
            for j in (way, 1 - way):
                pass_on(at(h, 0, 0, j), p1_rs.at[four(way, h, j)], near(h, 1 - 2 * way, 0))
    for h in range(2):
        for j in range(2):
            share(at(h, 0, 0, j))

    def second_axis(g, du, h, j):
        for way in range(2):
            pass_on(at(h, du, 0, j), q1_rs.at[g * 8 + four(way, h, j)], near(h, 0, 1 - 2 * way))

    for h in range(2):
        for j in range(2):
            second_axis(0, 0, h, j)
    for way in range(2):
        du = 2 * way - 1
        for h in range(2):
            for j in (way, 1 - way):
                block = at(h, du, 0, j)
                wait(grads.at[block], p1_rs.at[four(way, h, j)])
                if j == way:
                    pass_on(block, p2_rs.at[2 * h + way], near(h, 1 - 2 * way, 0))
                second_axis(1 + way, du, h, j)
                share(block)
    for h in range(2):
        for j in range(2):
            block = at(h, 2, 0, j)
            wait(grads.at[block], p2_rs.at[2 * h + j])
            second_axis(3, 2, h, j)
            share(block)

    acc = wgp[slab(z, core), :] + wgc_recv[z]
    for d in range(1, FEAT):
        zz = along_z(d)
        wait(wgz_recv.at[zz], wgz_rs.at[zz])
        acc = acc + wgz_recv[zz].astype(f32)
    tiles = [acc[8 * a : 8 * a + 8, 128 * b : 128 * b + 128] for a in range(6) for b in range(6)]
    for t in range(36):
        wx_send[t // 9, t % 9] = tiles[t]
    for d in range(1, SIDE):
        xx = around(x, d)
        send(wx_send.at[xx], wx_recv.at[x], wg_ss.at[2], wx_rs.at[x], near(0, d, 0))

    offs = (0, -1, 1, 2)

    def take(g):
        du = offs[g]
        for way in range(2):
            dv = 2 * way - 1
            for h in range(2):
                for j in (way, 1 - way):
                    block = at(h, du, dv, j)
                    wait(grads.at[block], q1_rs.at[g * 8 + four(way, h, j)])
                    if j == way:
                        pass_on(block, q2_rs.at[g * 4 + 2 * h + way], near(h, 0, 1 - 2 * way))
                    share(block)

    take(0)
    total = wx_send[x]
    for d in range(1, SIDE):
        xx = around(x, d)
        wait(wx_recv.at[xx], wx_rs.at[xx])
        total = total + wx_recv[xx]
    wy_send[...] = total
    wy_recv[y] = total
    for d in range(1, SIDE):
        send(wy_send, wy_recv.at[y], wg_ss.at[3], wy_rs.at[y], near(1, d, 0))
    take(1)
    for d in range(1, SIDE):
        yy = around(y, d)
        wait(wy_recv.at[yy], wy_rs.at[yy])
    total = (wy_recv[0] + wy_recv[1]) + (wy_recv[2] + wy_recv[3])
    wf_send[...] = total
    wf_recv[x] = total
    for d in range(1, SIDE):
        send(wf_send, wf_recv.at[x], wg_ss.at[4], wf_rs.at[x], near(0, d, 0))
    take(2)
    for d in range(1, SIDE):
        xx = around(x, d)
        wait(wf_recv.at[xx], wf_rs.at[xx])
    for t in range(36):
        a, b = t // 6, t % 6
        wg_half[8 * a : 8 * a + 8, 128 * b : 128 * b + 128] = wf_recv[t // 9, t % 9]
    mine = pl.ds(pl.multiple_of(core * HALF, HALF), HALF)
    other = pl.ds(pl.multiple_of((1 - core) * HALF, HALF), HALF)
    send(wg_half, wg_out.at[mine, :], wg_ss.at[5], wl_rs, sibling)
    own_wg = pltpu.make_async_copy(wg_half, wg_out.at[mine, :], local_sem.at[2])
    own_wg.start()
    take(3)
    for g in range(4):
        for h in range(2):
            for j in range(2):
                block = at(h, offs[g], 2, j)
                wait(grads.at[block], q2_rs.at[g * 4 + 2 * h + j])
                share(block)

    own_wg.wait()
    wait(wg_out.at[other, :], wl_rs)
    own_act.wait()

    def act_in(d):
        zz = along_z(d)
        wait(act_out.at[:, pl.ds(pl.multiple_of(zz * CHUNK, CHUNK), CHUNK)], act_rs.at[zz])

    lax.fori_loop(1, FEAT, lambda d, c: (act_in(d), c)[1], 0)
    wait(grads.at[pl.ds(0, 64)], pair_rs)
    wait(grads.at[pl.ds(0, 124)], ag_ss)
    wait(sib_send, sib_ss)
    wait(s1_send, s1_ss)
    wait(s2_send, s2_ss)
    wait(t1_send, t_ss.at[0])
    wait(t2_send, t_ss.at[1])
    seven = pl.ds(0, (FEAT - 1) * W)
    wait(wfull.at[seven, :], z_ss.at[0])
    for k in range(1, 5):
        wait(cot_in.at[seven, :], z_ss.at[k])
    wait(wgc_recv, wg_ss.at[0])
    wait(wgz_send.at[pl.ds(0, FEAT - 1)], wg_ss.at[1])
    for k in (2, 3, 4):
        wait(wx_send.at[pl.ds(0, SIDE - 1)], wg_ss.at[k])
    wait(wg_half, wg_ss.at[5])


def exchange(table, msg, weight, cot):
    dma = pltpu.SemaphoreType.DMA
    block = (W, TILE)
    vmem = pltpu.VMEM
    any_spec = pl.BlockSpec(memory_space=pl.ANY)
    vmem_spec = pl.BlockSpec(memory_space=pltpu.VMEM)
    return pl.pallas_call(
        exchange_kernel,
        in_specs=[pl.BlockSpec(memory_space=pltpu.SMEM), vmem_spec, vmem_spec, vmem_spec],
        out_specs=[any_spec] * 3,
        out_shape=[
            jax.ShapeDtypeStruct(cot.shape, bf16),
            jax.ShapeDtypeStruct((W, D), f32),
            jax.ShapeDtypeStruct((BLOCKS, *block), bf16),
        ],
        scratch_shapes=[
            vmem((64, *block), bf16), vmem((64, *block), bf16),
            vmem((16, *block), bf16), vmem((16, *block), bf16),
            vmem((32, *block), bf16), vmem((32, *block), bf16),
            vmem((4, *block), bf16), vmem((4, *block), bf16),
            vmem((8, *block), bf16), vmem((8, *block), bf16),
            vmem((LB, *block), bf16),
            vmem((D, CHUNK), bf16), vmem((D, D), bf16), vmem((D, CHUNK), bf16),
            vmem((D, CHUNK), bf16), vmem((D, CHUNK), bf16), vmem((D, CHUNK), bf16),
            vmem((D, D), f32), vmem((FEAT, W // 2, D), f32),
            vmem((FEAT, W // 2, D), bf16), vmem((FEAT, W // 2, D), bf16),
            vmem((SIDE, 9, 8, 128), f32), vmem((SIDE, 9, 8, 128), f32),
            vmem((9, 8, 128), f32), vmem((SIDE, 9, 8, 128), f32),
            vmem((9, 8, 128), f32), vmem((SIDE, 9, 8, 128), f32),
            vmem((W // 2, D), f32),
            dma, dma((64,)), dma, dma((16,)), dma, dma((32,)), dma((2,)), dma((4,)), dma((8,)),
            dma((5,)), dma((FEAT,)), dma((FEAT,)), dma((FEAT,)), dma((FEAT,)), dma((FEAT,)), dma((3,)),
            dma, dma((8,)), dma((4,)), dma((32,)), dma((16,)), dma,
            dma((6,)), dma((FEAT,)), dma((FEAT,)), dma((SIDE,)), dma((SIDE,)), dma((SIDE,)), dma,
        ],
        compiler_params=pltpu.CompilerParams(
            collective_id=0, has_side_effects=True, vmem_limit_bytes=VMEM_LIMIT
        ),
    )(table, msg, weight, cot)


def local(features, pair_doc, pair_label, incidence, weight, cotangent):
    msg, table = forward_pairs(pair_doc, pair_label, features.T, incidence)
    act, weight_grad, grads = exchange(table, msg, weight, cotangent.T)
    feature_grad = backward_pairs(pair_doc, pair_label, grads, incidence, features.shape[0])
    return act.T, weight_grad, feature_grad.T


def solution(mesh):
    return jax.shard_map(
        local,
        mesh=mesh,
        in_specs=(
            P("rows", "feat"),
            P("rows"),
            P("rows"),
            P("rows", None, None),
            P("feat", None),
            P("rows", "feat"),
        ),
        out_specs=(P("rows", "feat"), P("feat", None), P("rows", "feat")),
        check_vma=False,
    )
```

time: 534 us -> 145 us (0.27)
  waiting for transfers between devices: 249 us -> 0 us
  Pallas kernels: 0 us -> 143 us
  blocking collectives: 120 us -> 0 us
  local copies, waits for them, and re-layouts: 102 us -> 1.47 us
  matrix products: 36 us -> 0 us
  between operations: 14.6 us -> 0.66 us
  starting transfers between devices: 9.24 us -> 0 us
    all_gather x4 -> x0, waiting for transfers between devices: 156 us -> none  [the longest x1 64.1 us: local(): every_block = lax.all_gather(grad_blocks, 'rows', axis=0, tiled=True)]
    pallas_call x0 -> x3, Pallas kernels: none -> 143 us  [the longest x1 122 us: exchange(): pl.pallas_call(exchange_kernel, in_specs=[pl.BlockSpec(memory_space=pltpu...]
    unnamed x1 -> x0, blocking collectives: 120 us -> none
    psum x1 -> x0, waiting for transfers between devices: 92.4 us -> none  [local(): weight_grad = lax.psum(weight_part, 'rows')]
    reshape x7 -> x0, local copies, waits for them, and re-layouts: 49.6 us -> none  [the longest x2 27.5 us: local(): outgoing.reshape(owner_count, CAPO * tile_rows, slice_width)]
    dot_general x7 -> x0, matrix products: 36 us -> none  [the longest x1 9.21 us: local(): jnp.einsum('pdl,plw->pdw', incidence, pair_grads, preferred_element_type=...]
    scatter x2 -> x0, local copies, waits for them, and re-layouts: 19.9 us -> none  [local(): outgoing = jnp.zeros((owner_count * CAPO, tile_rows, slice_width), jnp.bf...]
    all_to_all x1 -> x0, local copies, waits for them, and re-layouts: 14.6 us -> none  [local(): lax.all_to_all(outgoing.reshape(owner_count, CAPO * tile_rows, slice_widt...]
  transfers between devices with their start and end apart: 6 -> 0, of which waited for: 4 -> 0; matrix products, arithmetic and copies ran while one was open for 13% -> 0% of each run, Pallas kernels for 0% -> 0%
where the time goes in v1:
time: 145 us
  Pallas kernels  143 us (99%)
  local copies, waits for them, and re-layouts  1.47 us (1%)
    pallas_call x1, Pallas kernels, exchange(): pl.pallas_call(exchange_kernel, in_specs=[pl.BlockSpec(memory_space=pltpu...  122 us
    pallas_call x1, Pallas kernels, forward_pairs(): pl.pallas_call(forward_kernel, grid_spec=pltpu.PrefetchScalarGridSpec(num...  10.6 us
    pallas_call x1, Pallas kernels, backward_pairs(): pl.pallas_call(backward_kernel, grid_spec=pltpu.PrefetchScalarGridSpec(nu...  10.5 us

profile of v1, /device:TPU:1, one launch (start us, length us, event | category | flops | bytes accessed | tf_op | source)
XLA Modules:
  0.0 145.0 jit_solution(4029404963066342182)
XLA Ops:
  0.6 10.6 %shard_map.85 = (bf16[25,96,512]{2,1,0:T(8,128)(2,1)}, s32[384]{0:T(512)}) custom-call(s32[24]{0:T(128)} %doc_ref.3, s32[24]{0:T(128)} %label_ref.3, bf16[96,2048]{1,0:T(8,128)(2,1)} %bitcast.5, bf16[24,512,512]{2,1,0:T(8,128)(2,1)} %refs_4_.1), custom_call_target="tpu_custom_call" | custom-call | tf_op jit(solution)/shard_map/pallas_call | solution.py:62
  11.2 121.9 %shard_map.86 = (bf16[96,2048]{1,0:T(8,128)(2,1)}, f32[96,768]{1,0:T(8,128)}, bf16[128,96,512]{2,1,0:T(8,128)(2,1)}) custom-call(s32[384]{0:T(512)} %get-tuple-element.8.table, bf16[25,96,512]{2,1,0:T(8,128)(2,1)} %get-tuple-element.9.msg, bf16[96,768]{1,0:T(8,128)(2,1)} %weight.1, bf16[96,2048]{1,0:T(8,128)(2,1)} %bitcast.6), custom_call_target="tpu_custom_call" | custom-call | tf_op jit(solution)/shard_map/pallas_call | solution.py:530
  133.1 0.0 copy-start
  133.1 0.0 copy-start.1
  133.1 10.5 %shard_map.87 = bf16[96,2048]{1,0:T(8,128)(2,1)} custom-call(s32[24]{0:T(128)} %doc_ref.3, s32[24]{0:T(128)} %label_ref.3, bf16[128,96,512]{2,1,0:T(8,128)(2,1)} %get-tuple-element.12.refs_0_.refs_1_.refs_2_.refs_3_, bf16[128,96,512]{2,1,0:T(8,128)(2,1)} %get-tuple-element.12.refs_0_.refs_1_.refs_2_.refs_3_, ...), custom_call_target="tpu_custom_call" | custom-call | tf_op jit(solution)/shard_map/pallas_call | solution.py:110
  143.6 0.0 copy-done
  143.6 0.7 copy.11
  144.3 0.0 copy-done.1
  144.3 0.7 copy.12
Async XLA Ops:
  133.1 10.5 %copy-start = (bf16[96,2048]{1,0:T(8,128)(2,1)S(1)}, bf16[96,2048]{1,0:T(8,128)(2,1)}, u32[]{:S(2)}) copy-start(bf16[96,2048]{1,0:T(8,128)(2,1)} %get-tuple-element.10) | copy-start | bytes 1179652
  133.1 11.2 %copy-start.1 = (f32[96,768]{1,0:T(8,128)S(1)}, f32[96,768]{1,0:T(8,128)}, u32[]{:S(2)}) copy-start(f32[96,768]{1,0:T(8,128)} %get-tuple-element.17) | copy-start | bytes 884740

commit v2 on v0

v2 whole, which is shorter than its diff:
```python
import functools

import jax
import jax.numpy as jnp
from jax import lax
from jax.experimental import pallas as pl
from jax.experimental.pallas import tpu as pltpu
from jax.sharding import PartitionSpec as P

MESH = pl.DeviceIdType.MESH
message_scale = 0.0625

SIDE = 4
FEAT = 8
LB = 4
CAP = 3
TILE = 512
PAIRS = 24
W = 96
D = 768
GROUP = 4
BLOCKS = 128
CHUNK = 256
PART = 128
BATCHES = PAIRS // GROUP
NONE = 2 * PAIRS
VMEM_LIMIT = 60 * 1024 * 1024

f32, bf16 = jnp.float32, jnp.bfloat16


def backward_kernel(doc_ref, label_ref, *refs):
    grads, inc_ref, out_ref, acc = refs[:GROUP], refs[GROUP], refs[GROUP + 1], refs[GROUP + 2]
    step = pl.program_id(0)
    rows = lax.axis_index("rows")
    tiles = acc.shape[0]

    @pl.when(step == 0)
    def _():
        acc[...] = jnp.zeros_like(acc)

    for k in range(GROUP):
        tile = doc_ref[step * GROUP + k] - rows * tiles
        grad = jnp.concatenate([grads[k][0, 0], grads[k][1, 0]], axis=1)
        acc[tile] += lax.dot_general(
            grad, inc_ref[k], (((1,), (1,)), ((), ())), preferred_element_type=f32
        )

    @pl.when(step == PAIRS // GROUP - 1)
    def _():
        for t in range(tiles):
            out_ref[:, t * TILE : (t + 1) * TILE] = acc[t].astype(bf16)


def backward_pairs(doc, label, grads, inc, width):
    def pick(k):
        return lambda i, d, l: (0, l[i * GROUP + k], 0, 0)

    return pl.pallas_call(
        backward_kernel,
        grid_spec=pltpu.PrefetchScalarGridSpec(
            num_scalar_prefetch=2,
            grid=(PAIRS // GROUP,),
            in_specs=[pl.BlockSpec((2, 1, W, CHUNK), pick(k)) for k in range(GROUP)]
            + [pl.BlockSpec((GROUP, TILE, TILE), lambda i, d, l: (i, 0, 0))],
            out_specs=pl.BlockSpec((W, width), lambda i, d, l: (0, 0)),
            scratch_shapes=[pltpu.VMEM((width // TILE, W, TILE), f32)],
        ),
        out_shape=jax.ShapeDtypeStruct((W, width), bf16),
        compiler_params=pltpu.CompilerParams(vmem_limit_bytes=VMEM_LIMIT),
    )(doc, label, *([grads] * GROUP), inc)


def wait(ref, sem):
    pltpu.make_async_copy(ref, ref, sem).wait()


def offset(i):
    return 2 - i + 3 * (i // 2) - 2 * (i // 3)


def exchange_kernel(
    doc_ref, label_ref, feat, inc, weight, cot,
    act_out, wg_out, grads,
    tiles, inc_buf, msg_a, msg_b, tab, tab_out, tab_in, tab_own, tab_sib,
    s1_send, s1_recv, s2_send, s2_recv, t1_send, t1_recv, t2_send, t2_recv,
    summed, xin, wfull, cot_in, act_buf, gm_buf, gmt_buf,
    wgp, wgc_recv, wgz_send, wgz_recv, wx_send, wx_recv, wy_send, wy_recv, wf_send, wf_recv, wg_half,
    inc_sem, tab_sems, sib_ss, sib_rs, s1_ss, s1_rs, s2_ss, s2_rs, t_ss, t1_rs, t2_rs,
    z_ss, x_rs, w_rs, cot_rs, act_rs, gz_rs, local_sem,
    ag_ss, p1_rs, p2_rs, q1_rs, q2_rs, pair_rs,
    wg_ss, wgc_rs, wgz_rs, wx_rs, wy_rs, wf_rs, wl_rs,
):
    r, z = lax.axis_index("rows"), lax.axis_index("feat")
    core, x, y = lax.rem(r, 2), lax.rem(r // 2, SIDE), r // (2 * SIDE)

    def around(value, step):
        return lax.rem(value + step + 2 * SIDE, SIDE)

    def row_of(yy, xx, cc):
        return (yy * SIDE + xx) * 2 + cc

    place = ((x, y), (y, x))
    msg = (msg_a, msg_b)

    def owner(h, u, v, cc):
        return row_of(v, u, cc) if h == 0 else row_of(u, v, cc)

    def near(h, du, dv):
        u, v = place[h]
        return {"rows": owner(h, around(u, du), around(v, dv), core), "feat": z}

    sibling = {"rows": row_of(y, x, 1 - core), "feat": z}

    def along_z(d):
        return lax.rem(z + d, FEAT)

    def send(src, dst, ss, rs, target):
        pltpu.make_async_remote_copy(
            src_ref=src, dst_ref=dst, send_sem=ss, recv_sem=rs, device_id=target, device_id_type=MESH
        ).start()

    def loop(n, body, start=0):
        lax.fori_loop(start, n, lambda i, c: (body(i), c)[1], 0)

    def others(body):
        loop(FEAT, lambda d: body(along_z(d)), 1)

    barrier = pltpu.get_barrier_semaphore()
    partners = [sibling]
    for d in range(1, SIDE):
        partners += [near(0, d, 0), near(1, d, 0)]
    for d in range(1, FEAT):
        partners.append({"rows": r, "feat": along_z(d)})
    for target in partners:
        pl.semaphore_signal(barrier, inc=1, device_id=target, device_id_type=MESH)

    def inc_copy(g, b):
        return pltpu.make_async_copy(
            inc.at[pl.ds(b * GROUP, GROUP), :, pl.ds(g * CHUNK, CHUNK)],
            inc_buf.at[pl.ds((g * BATCHES + b) * GROUP, GROUP)],
            inc_sem.at[g * BATCHES + b],
        )

    for g in range(2):
        for b in range(BATCHES):
            inc_copy(g, b).start()

    lane = lax.broadcasted_iota(jnp.int32, (1, BLOCKS), 1)
    count = jnp.zeros((1, BLOCKS), jnp.int32)
    spots = [jnp.full((1, BLOCKS), NONE, jnp.int32) for _ in range(CAP)]
    for p in range(PAIRS):
        hit = lane == label_ref[p]
        spots = [jnp.where(hit & (count == k), p, spots[k]) for k in range(CAP)]
        count = count + jnp.where(hit, 1, 0)
    tab[...] = jnp.full(tab.shape, NONE, jnp.int32)
    tab_out[...] = jnp.full(tab.shape, NONE, jnp.int32)
    for k in range(CAP):
        tab[k : k + 1, :] = spots[k]
        tab_out[k : k + 1, :] = jnp.where(spots[k] < NONE, spots[k] + PAIRS, NONE)
    own_tab = pltpu.make_async_copy(tab, tab_own, tab_sems.at[0])
    own_tab.start()
    for t in range(feat.shape[1] // TILE):
        tiles[t] = feat[:, t * TILE : (t + 1) * TILE]
    for g in range(2):
        msg[g][NONE] = jnp.zeros((W, CHUNK), bf16)

    pl.semaphore_wait(barrier, len(partners))
    send(tab_out, tab_in, tab_sems.at[1], tab_sems.at[2], sibling)

    tile_count = feat.shape[1] // TILE

    def messages(g):
        def batch(b):
            inc_copy(g, b).wait()
            for k in range(GROUP):
                p = b * GROUP + k
                product = jnp.dot(
                    tiles[lax.rem(doc_ref[p], tile_count)], inc_buf[g * PAIRS + p], preferred_element_type=f32
                )
                msg[g][p] = (message_scale * product).astype(bf16)
            send(
                msg[g].at[pl.ds(b * GROUP, GROUP)], msg[g].at[pl.ds(PAIRS + b * GROUP, GROUP)],
                sib_ss.at[g], sib_rs.at[g * BATCHES + b], sibling,
            )

        loop(BATCHES, batch)

    def pair_messages_in(g):
        def one(b):
            wait(msg[g].at[pl.ds(PAIRS + b * GROUP, GROUP)], sib_rs.at[g * BATCHES + b])

        loop(BATCHES, one)

    def block_id(h, u, v, j, cc):
        return owner(h, u, v, cc) * LB + 2 * h + j

    def part(g, h, du, dv, j):
        u, v = place[h]
        block = block_id(h, around(u, du), around(v, dv), j, core)
        total = msg[g][tab_own[0, block]].astype(f32)
        for k in range(1, CAP):
            total = total + msg[g][tab_own[k, block]].astype(f32)
        for k in range(CAP):
            total = total + msg[g][tab_sib[k, block]].astype(f32)
        return total

    def slot(g, a, i, h, j):
        return (((a * 2 + g) * SIDE + i) * 2 + h) * 2 + j

    def far(g):
        def one(i):
            for h in range(2):
                for j in range(2):
                    k = slot(g, 0, i, h, j)
                    s1_send[k] = part(g, h, 2, offset(i), j).astype(bf16)
                    send(s1_send.at[k], s1_recv.at[k], s1_ss, s1_rs.at[k], near(h, 1 - 2 * j, 0))

        loop(SIDE, one)

    def close(g, passed):
        def one(i):
            for h in range(2):
                for way in range(2):
                    du = 1 - 2 * way
                    j = way if passed else 1 - way
                    k = slot(g, way, i, h, j)
                    total = part(g, h, du, offset(i), j)
                    if passed:
                        q = slot(g, 0, i, h, j)
                        wait(s1_recv.at[q], s1_rs.at[q])
                        total = total + s1_recv[q].astype(f32)
                    s2_send[k] = total.astype(bf16)
                    send(s2_send.at[k], s2_recv.at[k], s2_ss, s2_rs.at[k], near(h, du, 0))

        loop(SIDE, one)

    def column(g, i, h, j):
        total = part(g, h, 0, offset(i), j)
        for way in (1 - j, j):
            k = slot(g, way, i, h, j)
            wait(s2_recv.at[k], s2_rs.at[k])
            total = total + s2_recv[k].astype(f32)
        return total

    def four(way, h, j):
        return (way * 2 + h) * 2 + j

    def second_axis_sums(g):
        for h in range(2):
            for j in range(2):
                k = 4 * g + 2 * h + j
                t1_send[k] = column(g, 0, h, j).astype(bf16)
                send(t1_send.at[k], t1_recv.at[k], t_ss.at[0], t1_rs.at[k], near(h, 0, 1 - 2 * j))
        for passed in (False, True):
            for way in range(2):
                for h in range(2):
                    j = way if passed else 1 - way
                    k = 8 * g + four(way, h, j)
                    total = column(g, 1 + way, h, j)
                    if passed:
                        q = 4 * g + 2 * h + j
                        wait(t1_recv.at[q], t1_rs.at[q])
                        total = total + t1_recv[q].astype(f32)
                    t2_send[k] = total.astype(bf16)
                    send(t2_send.at[k], t2_recv.at[k], t_ss.at[1], t2_rs.at[k], near(h, 0, 1 - 2 * way))

    own_rows = pl.ds(pl.multiple_of(z * W, W), W)

    def rows_at(zz):
        return pl.ds(pl.multiple_of(zz * W, W), W)

    def lanes_in_block(zz, base=0):
        return pl.ds(pl.multiple_of(base + lax.rem(zz, 2) * PART, PART), PART)

    def lanes_in_all(zz, g):
        return pl.ds(pl.multiple_of((zz // 2) * TILE + g * CHUNK + lax.rem(zz, 2) * PART, PART), PART)

    def group_lanes(g):
        return pl.ds(g * PART, PART)

    def to(zz):
        return {"rows": r, "feat": zz}

    def finish_sums(g):
        for h in range(2):
            for j in range(2):
                total = column(g, 3, h, j)
                for way in (1 - j, j):
                    k = 8 * g + four(way, h, j)
                    wait(t2_recv.at[k], t2_rs.at[k])
                    total = total + t2_recv[k].astype(f32)
                summed[g * LB + 2 * h + j] = total.astype(bf16)

        def one(zz):
            send(summed.at[g * LB + zz // 2, :, lanes_in_block(zz)], xin.at[own_rows, group_lanes(g)],
                 z_ss.at[2], x_rs.at[g * FEAT + z], to(zz))

        others(one)
        xin[own_rows, group_lanes(g)] = summed[g * LB + z // 2, :, lanes_in_block(z)]

    def background():
        def one(zz):
            send(weight, wfull.at[own_rows, :], z_ss.at[0], w_rs.at[z], to(zz))
            for g in range(2):
                send(cot.at[:, lanes_in_all(zz, g)], cot_in.at[own_rows, group_lanes(g)],
                     z_ss.at[1], cot_rs.at[g * FEAT + z], to(zz))

        others(one)
        wfull[own_rows, :] = weight[...]
        for g in range(2):
            cot_in[own_rows, group_lanes(g)] = cot[:, lanes_in_all(z, g)]

    own_copies = []

    def mix(g):
        if g == 0:
            others(lambda zz: wait(wfull.at[rows_at(zz), :], w_rs.at[zz]))
            for gg in range(2):
                others(lambda zz: wait(cot_in.at[rows_at(zz), group_lanes(gg)], cot_rs.at[gg * FEAT + zz]))
        others(lambda zz: wait(xin.at[rows_at(zz), group_lanes(g)], x_rs.at[g * FEAT + zz]))

        def forth(o):
            rows = pl.ds(pl.multiple_of(o * CHUNK, CHUNK), CHUNK)
            mixed = lax.dot_general(
                wfull[:, rows], xin[:, group_lanes(g)], (((0,), (0,)), ((), ())), preferred_element_type=f32
            )
            gate = jax.nn.sigmoid(mixed)
            act_buf[rows, group_lanes(g)] = (mixed * gate).astype(bf16)
            slope = gate * (1.0 + mixed * (1.0 - gate))
            gm_buf[rows, group_lanes(g)] = (cot_in[rows, group_lanes(g)].astype(f32) * slope).astype(bf16)

        loop(D // CHUNK, forth)

        def back(o):
            rows = pl.ds(pl.multiple_of(o * CHUNK, CHUNK), CHUNK)
            gmt_buf[rows, group_lanes(g)] = jnp.dot(
                wfull[rows, :], gm_buf[:, group_lanes(g)], preferred_element_type=f32
            ).astype(bf16)

        loop(D // CHUNK, back)
        mine = grads.at[g, r * LB + z // 2, :, lanes_in_block(z)]
        others(lambda zz: send(gmt_buf.at[rows_at(zz), group_lanes(g)], mine, z_ss.at[3], gz_rs.at[g * FEAT + z], to(zz)))
        own = pltpu.make_async_copy(gmt_buf.at[own_rows, group_lanes(g)], mine, local_sem.at[g])
        own.start()
        there = act_out.at[:, lanes_in_all(z, g)]
        others(lambda zz: send(act_buf.at[rows_at(zz), group_lanes(g)], there, z_ss.at[4], act_rs.at[g * FEAT + z], to(zz)))
        own_act = pltpu.make_async_copy(act_buf.at[own_rows, group_lanes(g)], there, local_sem.at[2 + g])
        own_act.start()
        own_copies.append((own, own_act))

    def share(g, block):
        send(grads.at[g, block], grads.at[g, block], ag_ss, pair_rs, sibling)

    def pass_on(g, block, rs, target):
        send(grads.at[g, block], grads.at[g, block], ag_ss, rs, target)

    def at(h, du, dv, j):
        u, v = place[h]
        return block_id(h, around(u, du), around(v, dv), j, core)

    def second_axis(g, n, du, h, j):
        for way in range(2):
            pass_on(g, at(h, du, 0, j), q1_rs.at[g * 32 + n * 8 + four(way, h, j)], near(h, 0, 1 - 2 * way))

    def gather_own(g):
        own_copies[g][0].wait()
        others(lambda zz: wait(grads.at[g, r * LB + zz // 2, :, lanes_in_block(zz)], gz_rs.at[g * FEAT + zz]))
        for way in range(2):
            for h in range(2):
                for j in (way, 1 - way):
                    pass_on(g, at(h, 0, 0, j), p1_rs.at[8 * g + four(way, h, j)], near(h, 1 - 2 * way, 0))
        for h in range(2):
            for j in range(2):
                second_axis(g, 0, 0, h, j)
                share(g, at(h, 0, 0, j))

    def gather_near(g):
        for turn in range(2):
            for way in range(2):
                j = way if turn == 0 else 1 - way
                du = 2 * way - 1
                for h in range(2):
                    block = at(h, du, 0, j)
                    wait(grads.at[g, block], p1_rs.at[8 * g + four(way, h, j)])
                    if j == way:
                        pass_on(g, block, p2_rs.at[4 * g + 2 * h + way], near(h, 1 - 2 * way, 0))
                    second_axis(g, 1 + way, du, h, j)
                    share(g, block)

    def gather_far(g):
        for h in range(2):
            for j in range(2):
                block = at(h, 2, 0, j)
                wait(grads.at[g, block], p2_rs.at[4 * g + 2 * h + j])
                second_axis(g, 3, 2, h, j)
                share(g, block)

    offs = (0, -1, 1, 2)

    def take(g, n):
        for way in range(2):
            for h in range(2):
                for j in (way, 1 - way):
                    block = at(h, offs[n], 2 * way - 1, j)
                    wait(grads.at[g, block], q1_rs.at[g * 32 + n * 8 + four(way, h, j)])
                    if j == way:
                        pass_on(g, block, q2_rs.at[g * 16 + n * 4 + 2 * h + way], near(h, 0, 1 - 2 * way))
                    share(g, block)

    def take_last(g):
        for n in range(4):
            for h in range(2):
                for j in range(2):
                    block = at(h, offs[n], 2, j)
                    wait(grads.at[g, block], q2_rs.at[g * 16 + n * 4 + 2 * h + j])
                    share(g, block)

    HALF = W // 2

    def slab(s, cc):
        return pl.ds(pl.multiple_of(s * W + cc * HALF, HALF), HALF)

    def weight_terms():
        def one(s):
            rows = pl.ds(pl.multiple_of(s * CHUNK, CHUNK), CHUNK)
            wgp[rows, :] = lax.dot_general(
                xin[rows, :], gm_buf[...], (((1,), (1,)), ((), ())), preferred_element_type=f32
            )

        loop(D // CHUNK, one)
        loop(FEAT, lambda s: send(wgp.at[slab(s, 1 - core), :], wgc_recv.at[s], wg_ss.at[0], wgc_rs.at[s], sibling))

    def weight_to_z():
        def one(zz):
            wait(wgc_recv.at[zz], wgc_rs.at[zz])
            wgz_send[zz] = (wgp[slab(zz, core), :] + wgc_recv[zz]).astype(bf16)
            send(wgz_send.at[zz], wgz_recv.at[z], wg_ss.at[1], wgz_rs.at[z], to(zz))

        others(one)
        wait(wgc_recv.at[z], wgc_rs.at[z])

    def weight_to_x():
        wg_half[...] = wgp[slab(z, core), :] + wgc_recv[z]

        def one(zz):
            wait(wgz_recv.at[zz], wgz_rs.at[zz])
            wg_half[...] += wgz_recv[zz].astype(f32)

        others(one)
        for t in range(36):
            a, b = t // 6, t % 6
            wx_send[t // 9, t % 9] = wg_half[8 * a : 8 * a + 8, 128 * b : 128 * b + 128]
        for d in range(1, SIDE):
            xx = around(x, d)
            send(wx_send.at[xx], wx_recv.at[x], wg_ss.at[2], wx_rs.at[x], near(0, d, 0))

    def weight_to_y():
        total = wx_send[x]
        for d in range(1, SIDE):
            xx = around(x, d)
            wait(wx_recv.at[xx], wx_rs.at[xx])
            total = total + wx_recv[xx]
        wy_send[...] = total
        wy_recv[y] = total
        for d in range(1, SIDE):
            send(wy_send, wy_recv.at[y], wg_ss.at[3], wy_rs.at[y], near(1, d, 0))

    def weight_back_x():
        for d in range(1, SIDE):
            yy = around(y, d)
            wait(wy_recv.at[yy], wy_rs.at[yy])
        total = (wy_recv[0] + wy_recv[1]) + (wy_recv[2] + wy_recv[3])
        wf_send[...] = total
        wf_recv[x] = total
        for d in range(1, SIDE):
            send(wf_send, wf_recv.at[x], wg_ss.at[4], wf_rs.at[x], near(0, d, 0))

    mine = pl.ds(pl.multiple_of(core * HALF, HALF), HALF)
    other = pl.ds(pl.multiple_of((1 - core) * HALF, HALF), HALF)
    own_wg = pltpu.make_async_copy(wg_half, wg_out.at[mine, :], local_sem.at[4])

    def weight_done():
        for d in range(1, SIDE):
            xx = around(x, d)
            wait(wf_recv.at[xx], wf_rs.at[xx])
        for t in range(36):
            a, b = t // 6, t % 6
            wg_half[8 * a : 8 * a + 8, 128 * b : 128 * b + 128] = wf_recv[t // 9, t % 9]
        send(wg_half, wg_out.at[mine, :], wg_ss.at[5], wl_rs, sibling)
        own_wg.start()

    background()
    messages(0)
    wait(tab_in, tab_sems.at[2])
    sib_tab = pltpu.make_async_copy(tab_in, tab_sib, tab_sems.at[3])
    sib_tab.start()
    own_tab.wait()
    sib_tab.wait()
    pair_messages_in(0)
    far(0)
    close(0, False)
    messages(1)
    close(0, True)
    pair_messages_in(1)
    far(1)
    second_axis_sums(0)
    close(1, False)
    finish_sums(0)
    close(1, True)
    mix(0)
    second_axis_sums(1)
    gather_own(0)
    finish_sums(1)
    gather_near(0)
    mix(1)
    gather_far(0)
    weight_terms()
    take(0, 0)
    take(0, 1)
    gather_own(1)
    weight_to_z()
    take(0, 2)
    take(0, 3)
    gather_near(1)
    take_last(0)
    gather_far(1)
    weight_to_x()
    take(1, 0)
    weight_to_y()
    take(1, 1)
    weight_back_x()
    take(1, 2)
    weight_done()
    take(1, 3)
    take_last(1)

    own_wg.wait()
    wait(wg_out.at[other, :], wl_rs)
    for g in range(2):
        own_copies[g][1].wait()
        others(lambda zz: wait(act_out.at[:, lanes_in_all(zz, g)], act_rs.at[g * FEAT + zz]))
    for g in range(2):
        wait(msg[g].at[pl.ds(0, PAIRS)], sib_ss.at[g])
    wait(grads.at[:, pl.ds(0, 64)], pair_rs)
    wait(grads.at[:, pl.ds(0, 124)], ag_ss)
    wait(tab_out, tab_sems.at[1])
    wait(s1_send, s1_ss)
    wait(s2_send, s2_ss)
    wait(t1_send, t_ss.at[0])
    wait(t2_send, t_ss.at[1])
    seven = pl.ds(0, (FEAT - 1) * W)
    wait(wfull.at[seven, :], z_ss.at[0])
    for k in range(1, 5):
        wait(cot_in.at[seven, :], z_ss.at[k])
    wait(wgc_recv, wg_ss.at[0])
    wait(wgz_send.at[pl.ds(0, FEAT - 1)], wg_ss.at[1])
    for k in (2, 3, 4):
        wait(wx_send.at[pl.ds(0, SIDE - 1)], wg_ss.at[k])
    wait(wg_half, wg_ss.at[5])


def exchange(doc, label, feat, inc, weight, cot):
    dma = pltpu.SemaphoreType.DMA
    block = (W, CHUNK)
    vmem = pltpu.VMEM
    smem_spec = pl.BlockSpec(memory_space=pltpu.SMEM)
    any_spec = pl.BlockSpec(memory_space=pl.ANY)
    vmem_spec = pl.BlockSpec(memory_space=pltpu.VMEM)
    table = ((8, BLOCKS), jnp.int32)
    return pl.pallas_call(
        exchange_kernel,
        in_specs=[smem_spec, smem_spec, vmem_spec, any_spec, vmem_spec, vmem_spec],
        out_specs=[any_spec] * 3,
        out_shape=[
            jax.ShapeDtypeStruct(cot.shape, bf16),
            jax.ShapeDtypeStruct((W, D), f32),
            jax.ShapeDtypeStruct((2, BLOCKS, *block), bf16),
        ],
        scratch_shapes=[
            vmem((feat.shape[1] // TILE, W, TILE), bf16),
            vmem((2 * PAIRS, TILE, CHUNK), bf16), vmem((NONE + 1, *block), bf16), vmem((NONE + 1, *block), bf16),
            vmem(*table), vmem(*table), vmem(*table), pltpu.SMEM(*table), pltpu.SMEM(*table),
            vmem((32, *block), bf16), vmem((32, *block), bf16),
            vmem((64, *block), bf16), vmem((64, *block), bf16),
            vmem((8, *block), bf16), vmem((8, *block), bf16),
            vmem((16, *block), bf16), vmem((16, *block), bf16),
            vmem((2 * LB, *block), bf16),
            vmem((D, CHUNK), bf16), vmem((D, D), bf16), vmem((D, CHUNK), bf16),
            vmem((D, CHUNK), bf16), vmem((D, CHUNK), bf16), vmem((D, CHUNK), bf16),
            vmem((D, D), f32), vmem((FEAT, W // 2, D), f32),
            vmem((FEAT, W // 2, D), bf16), vmem((FEAT, W // 2, D), bf16),
            vmem((SIDE, 9, 8, 128), f32), vmem((SIDE, 9, 8, 128), f32),
            vmem((9, 8, 128), f32), vmem((SIDE, 9, 8, 128), f32),
            vmem((9, 8, 128), f32), vmem((SIDE, 9, 8, 128), f32),
            vmem((W // 2, D), f32),
            dma((2 * BATCHES,)), dma((4,)), dma((2,)), dma((2 * BATCHES,)),
            dma, dma((32,)), dma, dma((64,)), dma((2,)), dma((8,)), dma((16,)),
            dma((5,)), dma((2 * FEAT,)), dma((FEAT,)), dma((2 * FEAT,)), dma((2 * FEAT,)), dma((2 * FEAT,)), dma((5,)),
            dma, dma((16,)), dma((8,)), dma((64,)), dma((32,)), dma,
            dma((6,)), dma((FEAT,)), dma((FEAT,)), dma((SIDE,)), dma((SIDE,)), dma((SIDE,)), dma,
        ],
        compiler_params=pltpu.CompilerParams(
            collective_id=0, has_side_effects=True, vmem_limit_bytes=VMEM_LIMIT
        ),
    )(doc, label, feat, inc, weight, cot)


def local(features, pair_doc, pair_label, incidence, weight, cotangent):
    act, weight_grad, grads = exchange(
        pair_doc, pair_label, features.T, incidence, weight, cotangent.T
    )
    feature_grad = backward_pairs(pair_doc, pair_label, grads, incidence, features.shape[0])
    return act.T, weight_grad, feature_grad.T


def solution(mesh):
    return jax.shard_map(
        local,
        mesh=mesh,
        in_specs=(
            P("rows", "feat"),
            P("rows"),
            P("rows"),
            P("rows", None, None),
            P("feat", None),
            P("rows", "feat"),
        ),
        out_specs=(P("rows", "feat"), P("feat", None), P("rows", "feat")),
        check_vma=False,
    )
```

time: 534 us -> 128 us (0.24)
  waiting for transfers between devices: 249 us -> 0 us
  Pallas kernels: 0 us -> 126 us
  blocking collectives: 120 us -> 0 us
  local copies, waits for them, and re-layouts: 102 us -> 1.47 us
  matrix products: 36 us -> 0 us
  between operations: 14.6 us -> 0.66 us
  starting transfers between devices: 9.24 us -> 0 us
    all_gather x4 -> x0, waiting for transfers between devices: 156 us -> none  [the longest x1 64.1 us: local(): every_block = lax.all_gather(grad_blocks, 'rows', axis=0, tiled=True)]
    pallas_call x0 -> x2, Pallas kernels: none -> 126 us  [the longest x1 116 us: exchange(): pl.pallas_call(exchange_kernel, in_specs=[smem_spec, smem_spec, vmem_spec...]
    unnamed x1 -> x0, blocking collectives: 120 us -> none
    psum x1 -> x0, waiting for transfers between devices: 92.4 us -> none  [local(): weight_grad = lax.psum(weight_part, 'rows')]
    reshape x7 -> x0, local copies, waits for them, and re-layouts: 49.6 us -> none  [the longest x2 27.5 us: local(): outgoing.reshape(owner_count, CAPO * tile_rows, slice_width)]
    dot_general x7 -> x0, matrix products: 36 us -> none  [the longest x1 9.21 us: local(): jnp.einsum('pdl,plw->pdw', incidence, pair_grads, preferred_element_type=...]
    scatter x2 -> x0, local copies, waits for them, and re-layouts: 19.9 us -> none  [local(): outgoing = jnp.zeros((owner_count * CAPO, tile_rows, slice_width), jnp.bf...]
    all_to_all x1 -> x0, local copies, waits for them, and re-layouts: 14.6 us -> none  [local(): lax.all_to_all(outgoing.reshape(owner_count, CAPO * tile_rows, slice_widt...]
  transfers between devices with their start and end apart: 6 -> 0, of which waited for: 4 -> 0; matrix products, arithmetic and copies ran while one was open for 13% -> 0% of each run, Pallas kernels for 0% -> 0%
where the time goes in v2:
time: 128 us
  Pallas kernels  126 us (98%)
  local copies, waits for them, and re-layouts  1.47 us (1%)
    pallas_call x1, Pallas kernels, exchange(): pl.pallas_call(exchange_kernel, in_specs=[smem_spec, smem_spec, vmem_spec...  116 us
    pallas_call x1, Pallas kernels, backward_pairs(): pl.pallas_call(backward_kernel, grid_spec=pltpu.PrefetchScalarGridSpec(nu...  10.5 us

profile of v2, /device:TPU:1, one launch (start us, length us, event | category | flops | bytes accessed | tf_op | source)
XLA Modules:
  0.0 128.1 jit_solution(13317043468715363511)
XLA Ops:
  0.6 115.5 %shard_map.85 = (bf16[96,2048]{1,0:T(8,128)(2,1)}, f32[96,768]{1,0:T(8,128)}, bf16[2,128,96,256]{3,2,1,0:T(8,128)(2,1)}) custom-call(s32[24]{0:T(128)} %doc_ref.3, s32[24]{0:T(128)} %label_ref.3, bf16[96,2048]{1,0:T(8,128)(2,1)} %bitcast.5, bf16[24,512,512]{2,1,0:T(8,128)(2,1)} %refs_4_.1, bf16[96,768]{1,0:T(8,128)(2,1)} %weight.1, bf16[96,2048]{1,0:T(8,128)(2,1)} %bitcast.6), custom_call_target="tpu_custom_call" | custom-call | tf_op jit(solution)/shard_map/pallas_call | solution.py:571
  116.1 0.0 copy-start
  116.2 0.0 copy-start.1
  116.2 10.5 %shard_map.86 = bf16[96,2048]{1,0:T(8,128)(2,1)} custom-call(s32[24]{0:T(128)} %doc_ref.3, s32[24]{0:T(128)} %label_ref.3, bf16[2,128,96,256]{3,2,1,0:T(8,128)(2,1)} %get-tuple-element.8.refs_0_.refs_1_.refs_2_.refs_3_, bf16[2,128,96,256]{3,2,1,0:T(8,128)(2,1)} %get-tuple-element.8.refs_0_.refs_1_.refs_2_.refs_3_, ...), custom_call_target="tpu_custom_call" | custom-call | tf_op jit(solution)/shard_map/pallas_call | solution.py:59
  126.7 0.0 copy-done
  126.7 0.7 copy.11
  127.4 0.0 copy-done.1
  127.4 0.7 copy.12
Async XLA Ops:
  116.1 10.5 %copy-start = (bf16[96,2048]{1,0:T(8,128)(2,1)S(1)}, bf16[96,2048]{1,0:T(8,128)(2,1)}, u32[]{:S(2)}) copy-start(bf16[96,2048]{1,0:T(8,128)(2,1)} %get-tuple-element.6) | copy-start | bytes 1179652
  116.2 11.3 %copy-start.1 = (f32[96,768]{1,0:T(8,128)S(1)}, f32[96,768]{1,0:T(8,128)}, u32[]{:S(2)}) copy-start(f32[96,768]{1,0:T(8,128)} %get-tuple-element.13) | copy-start | bytes 884740

commit v3 on v2

--- a/solution.py
+++ b/solution.py
@@ -29,48 +29,6 @@
 f32, bf16 = jnp.float32, jnp.bfloat16
 
 
-def backward_kernel(doc_ref, label_ref, *refs):
-    grads, inc_ref, out_ref, acc = refs[:GROUP], refs[GROUP], refs[GROUP + 1], refs[GROUP + 2]
-    step = pl.program_id(0)
-    rows = lax.axis_index("rows")
-    tiles = acc.shape[0]
-
-    @pl.when(step == 0)
-    def _():
-        acc[...] = jnp.zeros_like(acc)
-
-    for k in range(GROUP):
-        tile = doc_ref[step * GROUP + k] - rows * tiles
-        grad = jnp.concatenate([grads[k][0, 0], grads[k][1, 0]], axis=1)
-        acc[tile] += lax.dot_general(
-            grad, inc_ref[k], (((1,), (1,)), ((), ())), preferred_element_type=f32
-        )
-
-    @pl.when(step == PAIRS // GROUP - 1)
-    def _():
-        for t in range(tiles):
-            out_ref[:, t * TILE : (t + 1) * TILE] = acc[t].astype(bf16)
-
-
-def backward_pairs(doc, label, grads, inc, width):
-    def pick(k):
-        return lambda i, d, l: (0, l[i * GROUP + k], 0, 0)
-
-    return pl.pallas_call(
-        backward_kernel,
-        grid_spec=pltpu.PrefetchScalarGridSpec(
-            num_scalar_prefetch=2,
-            grid=(PAIRS // GROUP,),
-            in_specs=[pl.BlockSpec((2, 1, W, CHUNK), pick(k)) for k in range(GROUP)]
-            + [pl.BlockSpec((GROUP, TILE, TILE), lambda i, d, l: (i, 0, 0))],
-            out_specs=pl.BlockSpec((W, width), lambda i, d, l: (0, 0)),
-            scratch_shapes=[pltpu.VMEM((width // TILE, W, TILE), f32)],
-        ),
-        out_shape=jax.ShapeDtypeStruct((W, width), bf16),
-        compiler_params=pltpu.CompilerParams(vmem_limit_bytes=VMEM_LIMIT),
-    )(doc, label, *([grads] * GROUP), inc)
-
-
 def wait(ref, sem):
     pltpu.make_async_copy(ref, ref, sem).wait()
 
@@ -81,7 +39,8 @@
 
 def exchange_kernel(
     doc_ref, label_ref, feat, inc, weight, cot,
-    act_out, wg_out, grads,
+    act_out, wg_out, fg_out,
+    grads_a, grads_b, fg_acc,
     tiles, inc_buf, msg_a, msg_b, tab, tab_out, tab_in, tab_own, tab_sib,
     s1_send, s1_recv, s2_send, s2_recv, t1_send, t1_recv, t2_send, t2_recv,
     summed, xin, wfull, cot_in, act_buf, gm_buf, gmt_buf,
@@ -102,6 +61,7 @@
 
     place = ((x, y), (y, x))
     msg = (msg_a, msg_b)
+    grads = (grads_a, grads_b)
 
     def owner(h, u, v, cc):
         return row_of(v, u, cc) if h == 0 else row_of(u, v, cc)
@@ -299,15 +259,31 @@
         others(one)
         xin[own_rows, group_lanes(g)] = summed[g * LB + z // 2, :, lanes_in_block(z)]
 
-    def background():
+    def pass_weight(slab, step):
+        rows = rows_at(slab)
+        send(wfull.at[rows, :], wfull.at[rows, :], z_ss.at[0], w_rs.at[slab], to(lax.rem(z + step + FEAT, FEAT)))
+
+    def weight_start():
+        wfull[own_rows, :] = weight[...]
+        pass_weight(z, 1)
+        pass_weight(z, -1)
+
+    def weight_forward(n):
+        below, above = lax.rem(z - n + FEAT, FEAT), lax.rem(z + n, FEAT)
+        wait(wfull.at[rows_at(below), :], w_rs.at[below])
+        if n < FEAT // 2:
+            pass_weight(below, 1)
+            wait(wfull.at[rows_at(above), :], w_rs.at[above])
+            if n < FEAT // 2 - 1:
+                pass_weight(above, -1)
+
+    def spread_cotangent():
         def one(zz):
-            send(weight, wfull.at[own_rows, :], z_ss.at[0], w_rs.at[z], to(zz))
             for g in range(2):
                 send(cot.at[:, lanes_in_all(zz, g)], cot_in.at[own_rows, group_lanes(g)],
                      z_ss.at[1], cot_rs.at[g * FEAT + z], to(zz))
 
         others(one)
-        wfull[own_rows, :] = weight[...]
         for g in range(2):
             cot_in[own_rows, group_lanes(g)] = cot[:, lanes_in_all(z, g)]
 
@@ -315,7 +291,7 @@
 
     def mix(g):
         if g == 0:
-            others(lambda zz: wait(wfull.at[rows_at(zz), :], w_rs.at[zz]))
+            weight_forward(FEAT // 2)
             for gg in range(2):
                 others(lambda zz: wait(cot_in.at[rows_at(zz), group_lanes(gg)], cot_rs.at[gg * FEAT + zz]))
         others(lambda zz: wait(xin.at[rows_at(zz), group_lanes(g)], x_rs.at[g * FEAT + zz]))
@@ -339,21 +315,26 @@
             ).astype(bf16)
 
         loop(D // CHUNK, back)
-        mine = grads.at[g, r * LB + z // 2, :, lanes_in_block(z)]
+        mine = grads[g].at[r * LB + z // 2, :, lanes_in_block(z)]
         others(lambda zz: send(gmt_buf.at[rows_at(zz), group_lanes(g)], mine, z_ss.at[3], gz_rs.at[g * FEAT + z], to(zz)))
         own = pltpu.make_async_copy(gmt_buf.at[own_rows, group_lanes(g)], mine, local_sem.at[g])
         own.start()
+        own_copies.append(own)
+
+    own_acts = []
+
+    def give_act(g):
         there = act_out.at[:, lanes_in_all(z, g)]
         others(lambda zz: send(act_buf.at[rows_at(zz), group_lanes(g)], there, z_ss.at[4], act_rs.at[g * FEAT + z], to(zz)))
         own_act = pltpu.make_async_copy(act_buf.at[own_rows, group_lanes(g)], there, local_sem.at[2 + g])
         own_act.start()
-        own_copies.append((own, own_act))
+        own_acts.append(own_act)
 
     def share(g, block):
-        send(grads.at[g, block], grads.at[g, block], ag_ss, pair_rs, sibling)
+        send(grads[g].at[block], grads[g].at[block], ag_ss.at[g], pair_rs.at[g], sibling)
 
     def pass_on(g, block, rs, target):
-        send(grads.at[g, block], grads.at[g, block], ag_ss, rs, target)
+        send(grads[g].at[block], grads[g].at[block], ag_ss.at[g], rs, target)
 
     def at(h, du, dv, j):
         u, v = place[h]
@@ -364,8 +345,8 @@
             pass_on(g, at(h, du, 0, j), q1_rs.at[g * 32 + n * 8 + four(way, h, j)], near(h, 0, 1 - 2 * way))
 
     def gather_own(g):
-        own_copies[g][0].wait()
-        others(lambda zz: wait(grads.at[g, r * LB + zz // 2, :, lanes_in_block(zz)], gz_rs.at[g * FEAT + zz]))
+        own_copies[g].wait()
+        others(lambda zz: wait(grads[g].at[r * LB + zz // 2, :, lanes_in_block(zz)], gz_rs.at[g * FEAT + zz]))
         for way in range(2):
             for h in range(2):
                 for j in (way, 1 - way):
@@ -382,7 +363,7 @@
                 du = 2 * way - 1
                 for h in range(2):
                     block = at(h, du, 0, j)
-                    wait(grads.at[g, block], p1_rs.at[8 * g + four(way, h, j)])
+                    wait(grads[g].at[block], p1_rs.at[8 * g + four(way, h, j)])
                     if j == way:
                         pass_on(g, block, p2_rs.at[4 * g + 2 * h + way], near(h, 1 - 2 * way, 0))
                     second_axis(g, 1 + way, du, h, j)
@@ -392,7 +373,7 @@
         for h in range(2):
             for j in range(2):
                 block = at(h, 2, 0, j)
-                wait(grads.at[g, block], p2_rs.at[4 * g + 2 * h + j])
+                wait(grads[g].at[block], p2_rs.at[4 * g + 2 * h + j])
                 second_axis(g, 3, 2, h, j)
                 share(g, block)
 
@@ -403,7 +384,7 @@
             for h in range(2):
                 for j in (way, 1 - way):
                     block = at(h, offs[n], 2 * way - 1, j)
-                    wait(grads.at[g, block], q1_rs.at[g * 32 + n * 8 + four(way, h, j)])
+                    wait(grads[g].at[block], q1_rs.at[g * 32 + n * 8 + four(way, h, j)])
                     if j == way:
                         pass_on(g, block, q2_rs.at[g * 16 + n * 4 + 2 * h + way], near(h, 0, 1 - 2 * way))
                     share(g, block)
@@ -413,8 +394,35 @@
             for h in range(2):
                 for j in range(2):
                     block = at(h, offs[n], 2, j)
-                    wait(grads.at[g, block], q2_rs.at[g * 16 + n * 4 + 2 * h + j])
+                    wait(grads[g].at[block], q2_rs.at[g * 16 + n * 4 + 2 * h + j])
                     share(g, block)
+
+    def backward_ready(g):
+        wait(grads[g].at[pl.ds(0, 64)], pair_rs.at[g])
+
+    def backward(g, first, last):
+        def batch(b):
+            left, right = [], []
+            for k in range(GROUP):
+                p = b * GROUP + k
+                grad = grads[g][label_ref[p]]
+                tile = lax.rem(doc_ref[p], tile_count)
+                left.append(
+                    jnp.concatenate(
+                        [jnp.where(tile == t, grad, jnp.zeros_like(grad)) for t in range(tile_count)], axis=0
+                    )
+                )
+                right.append(inc_buf[g * PAIRS + p])
+            fg_acc[...] += lax.dot_general(
+                jnp.concatenate(left, axis=1), jnp.concatenate(right, axis=1),
+                (((1,), (1,)), ((), ())), preferred_element_type=f32,
+            )
+
+        loop(last, batch, first)
+
+    def backward_done():
+        for t in range(tile_count):
+            fg_out[:, t * TILE : (t + 1) * TILE] = fg_acc[t * W : (t + 1) * W, :].astype(bf16)
 
     HALF = W // 2
 
@@ -490,7 +498,7 @@
         send(wg_half, wg_out.at[mine, :], wg_ss.at[5], wl_rs, sibling)
         own_wg.start()
 
-    background()
+    weight_start()
     messages(0)
     wait(tab_in, tab_sems.at[2])
     sib_tab = pltpu.make_async_copy(tab_in, tab_sib, tab_sems.at[3])
@@ -498,8 +506,12 @@
     own_tab.wait()
     sib_tab.wait()
     pair_messages_in(0)
+    weight_forward(1)
     far(0)
+    weight_forward(2)
     close(0, False)
+    weight_forward(3)
+    spread_cotangent()
     messages(1)
     close(0, True)
     pair_messages_in(1)
@@ -513,37 +525,45 @@
     gather_own(0)
     finish_sums(1)
     gather_near(0)
+    gather_far(0)
     mix(1)
-    gather_far(0)
-    weight_terms()
     take(0, 0)
     take(0, 1)
+    weight_terms()
+    take(0, 2)
+    take(0, 3)
     gather_own(1)
     weight_to_z()
-    take(0, 2)
-    take(0, 3)
+    give_act(0)
+    give_act(1)
+    fg_acc[...] = jnp.zeros_like(fg_acc)
+    take_last(0)
     gather_near(1)
-    take_last(0)
     gather_far(1)
+    backward_ready(0)
+    backward(0, 0, 3)
+    take(1, 0)
+    backward(0, 3, 6)
     weight_to_x()
-    take(1, 0)
+    take(1, 1)
+    take(1, 2)
     weight_to_y()
-    take(1, 1)
+    take(1, 3)
     weight_back_x()
-    take(1, 2)
+    take_last(1)
     weight_done()
-    take(1, 3)
-    take_last(1)
+    backward_ready(1)
+    backward(1, 0, BATCHES)
+    backward_done()
 
     own_wg.wait()
     wait(wg_out.at[other, :], wl_rs)
     for g in range(2):
-        own_copies[g][1].wait()
+        own_acts[g].wait()
         others(lambda zz: wait(act_out.at[:, lanes_in_all(zz, g)], act_rs.at[g * FEAT + zz]))
     for g in range(2):
         wait(msg[g].at[pl.ds(0, PAIRS)], sib_ss.at[g])
-    wait(grads.at[:, pl.ds(0, 64)], pair_rs)
-    wait(grads.at[:, pl.ds(0, 124)], ag_ss)
+        wait(grads[g].at[pl.ds(0, 124)], ag_ss.at[g])
     wait(tab_out, tab_sems.at[1])
     wait(s1_send, s1_ss)
     wait(s2_send, s2_ss)
@@ -571,13 +591,15 @@
     return pl.pallas_call(
         exchange_kernel,
         in_specs=[smem_spec, smem_spec, vmem_spec, any_spec, vmem_spec, vmem_spec],
-        out_specs=[any_spec] * 3,
+        out_specs=[any_spec, any_spec, vmem_spec],
         out_shape=[
             jax.ShapeDtypeStruct(cot.shape, bf16),
             jax.ShapeDtypeStruct((W, D), f32),
-            jax.ShapeDtypeStruct((2, BLOCKS, *block), bf16),
+            jax.ShapeDtypeStruct(feat.shape, bf16),
         ],
         scratch_shapes=[
+            vmem((BLOCKS, *block), bf16), vmem((BLOCKS, *block), bf16),
+            vmem((feat.shape[1] // TILE * W, TILE), f32),
             vmem((feat.shape[1] // TILE, W, TILE), bf16),
             vmem((2 * PAIRS, TILE, CHUNK), bf16), vmem((NONE + 1, *block), bf16), vmem((NONE + 1, *block), bf16),
             vmem(*table), vmem(*table), vmem(*table), pltpu.SMEM(*table), pltpu.SMEM(*table),
@@ -597,7 +619,7 @@
             dma((2 * BATCHES,)), dma((4,)), dma((2,)), dma((2 * BATCHES,)),
             dma, dma((32,)), dma, dma((64,)), dma((2,)), dma((8,)), dma((16,)),
             dma((5,)), dma((2 * FEAT,)), dma((FEAT,)), dma((2 * FEAT,)), dma((2 * FEAT,)), dma((2 * FEAT,)), dma((5,)),
-            dma, dma((16,)), dma((8,)), dma((64,)), dma((32,)), dma,
+            dma((2,)), dma((16,)), dma((8,)), dma((64,)), dma((32,)), dma((2,)),
             dma((6,)), dma((FEAT,)), dma((FEAT,)), dma((SIDE,)), dma((SIDE,)), dma((SIDE,)), dma,
         ],
         compiler_params=pltpu.CompilerParams(
@@ -607,10 +629,9 @@
 
 
 def local(features, pair_doc, pair_label, incidence, weight, cotangent):
-    act, weight_grad, grads = exchange(
+    act, weight_grad, feature_grad = exchange(
         pair_doc, pair_label, features.T, incidence, weight, cotangent.T
     )
-    feature_grad = backward_pairs(pair_doc, pair_label, grads, incidence, features.shape[0])
     return act.T, weight_grad, feature_grad.T
 
 

time: 128 us -> 122 us (0.953)
  Pallas kernels: 126 us -> 116 us
  local copies, waits for them, and re-layouts: 1.47 us -> 5.23 us
    pallas_call x1 -> x0, Pallas kernels: 10.5 us -> none  [backward_pairs(): pl.pallas_call(backward_kernel, grid_spec=pltpu.PrefetchScalarGridSpec(nu...]
    unnamed x6 -> x3, local copies, waits for them, and re-layouts: 1.47 us -> 5.23 us
where the time goes in v3:
time: 122 us
  Pallas kernels  116 us (95%)
  local copies, waits for them, and re-layouts  5.23 us (4%)
    pallas_call x1, Pallas kernels, exchange(): pl.pallas_call(exchange_kernel, in_specs=[smem_spec, smem_spec, vmem_spec...  116 us
    unnamed x3, local copies, waits for them, and re-layouts  5.23 us

profile of v3, /device:TPU:1, one launch (start us, length us, event | category | flops | bytes accessed | tf_op | source)
XLA Modules:
  0.0 121.5 jit_solution(10397172497495351560)
XLA Ops:
  0.6 115.7 %shard_map.85 = (bf16[96,2048]{1,0:T(8,128)(2,1)}, f32[96,768]{1,0:T(8,128)}, bf16[96,2048]{1,0:T(8,128)(2,1)}) custom-call(s32[24]{0:T(128)} %doc_ref.1, s32[24]{0:T(128)} %label_ref.1, bf16[96,2048]{1,0:T(8,128)(2,1)} %bitcast.4, bf16[24,512,512]{2,1,0:T(8,128)(2,1)} %inc.1, bf16[96,768]{1,0:T(8,128)(2,1)} %weight.1, bf16[96,2048]{1,0:T(8,128)(2,1)} %bitcast.5), custom_call_target="tpu_custom_call" | custom-call | tf_op jit(solution)/shard_map/pallas_call | solution.py:591
  116.3 1.8 %copy.12 = bf16[2048,96]{0,1:T(8,128)(2,1)} copy(bf16[2048,96]{0,1:T(8,128)(2,1)} %bitcast.7) | data formatting | bytes 786432
  118.1 1.7 %copy.13 = f32[96,768]{1,0:T(8,128)} copy(f32[96,768]{1,0:T(8,128)} %get-tuple-element.13) | data formatting | bytes 589824
  119.8 1.8 %copy.14 = bf16[2048,96]{0,1:T(8,128)(2,1)} copy(bf16[2048,96]{0,1:T(8,128)(2,1)} %bitcast.6) | data formatting | bytes 786432

commit v4 on v3

--- a/solution.py
+++ b/solution.py
@@ -44,7 +44,7 @@
     tiles, inc_buf, msg_a, msg_b, tab, tab_out, tab_in, tab_own, tab_sib,
     s1_send, s1_recv, s2_send, s2_recv, t1_send, t1_recv, t2_send, t2_recv,
     summed, xin, wfull, cot_in, act_buf, gm_buf, gmt_buf,
-    wgp, wgc_recv, wgz_send, wgz_recv, wx_send, wx_recv, wy_send, wy_recv, wf_send, wf_recv, wg_half,
+    x_pair, gm_pair, wgz_send, wgz_recv, wx_send, wx_recv, wy_send, wy_recv, wf_send, wf_recv, wg_half,
     inc_sem, tab_sems, sib_ss, sib_rs, s1_ss, s1_rs, s2_ss, s2_rs, t_ss, t1_rs, t2_rs,
     z_ss, x_rs, w_rs, cot_rs, act_rs, gz_rs, local_sem,
     ag_ss, p1_rs, p2_rs, q1_rs, q2_rs, pair_rs,
@@ -259,23 +259,20 @@
         others(one)
         xin[own_rows, group_lanes(g)] = summed[g * LB + z // 2, :, lanes_in_block(z)]
 
-    def pass_weight(slab, step):
-        rows = rows_at(slab)
-        send(wfull.at[rows, :], wfull.at[rows, :], z_ss.at[0], w_rs.at[slab], to(lax.rem(z + step + FEAT, FEAT)))
+    half_cols = pl.ds(pl.multiple_of(core * (D // 2), D // 2), D // 2)
+    other_cols = pl.ds(pl.multiple_of((1 - core) * (D // 2), D // 2), D // 2)
 
     def weight_start():
+        others(lambda zz: send(weight.at[:, half_cols], wfull.at[own_rows, half_cols], z_ss.at[0], w_rs.at[z], to(zz)))
         wfull[own_rows, :] = weight[...]
-        pass_weight(z, 1)
-        pass_weight(z, -1)
-
-    def weight_forward(n):
-        below, above = lax.rem(z - n + FEAT, FEAT), lax.rem(z + n, FEAT)
-        wait(wfull.at[rows_at(below), :], w_rs.at[below])
-        if n < FEAT // 2:
-            pass_weight(below, 1)
-            wait(wfull.at[rows_at(above), :], w_rs.at[above])
-            if n < FEAT // 2 - 1:
-                pass_weight(above, -1)
+
+    def weight_share():
+        def one(zz):
+            half = wfull.at[rows_at(zz), half_cols]
+            wait(half, w_rs.at[zz])
+            send(half, half, z_ss.at[5], w_rs.at[FEAT + zz], sibling)
+
+        others(one)
 
     def spread_cotangent():
         def one(zz):
@@ -291,7 +288,7 @@
 
     def mix(g):
         if g == 0:
-            weight_forward(FEAT // 2)
+            others(lambda zz: wait(wfull.at[rows_at(zz), other_cols], w_rs.at[FEAT + zz]))
             for gg in range(2):
                 others(lambda zz: wait(cot_in.at[rows_at(zz), group_lanes(gg)], cot_rs.at[gg * FEAT + zz]))
         others(lambda zz: wait(xin.at[rows_at(zz), group_lanes(g)], x_rs.at[g * FEAT + zz]))
@@ -429,28 +426,32 @@
     def slab(s, cc):
         return pl.ds(pl.multiple_of(s * W + cc * HALF, HALF), HALF)
 
-    def weight_terms():
-        def one(s):
-            rows = pl.ds(pl.multiple_of(s * CHUNK, CHUNK), CHUNK)
-            wgp[rows, :] = lax.dot_general(
-                xin[rows, :], gm_buf[...], (((1,), (1,)), ((), ())), preferred_element_type=f32
-            )
-
-        loop(D // CHUNK, one)
-        loop(FEAT, lambda s: send(wgp.at[slab(s, 1 - core), :], wgc_recv.at[s], wg_ss.at[0], wgc_rs.at[s], sibling))
+    def weight_inputs(g):
+        lanes = group_lanes(g)
+        send(xin.at[:, lanes], x_pair.at[:, lanes], wg_ss.at[0], wgc_rs.at[2 * g], sibling)
+        send(gm_buf.at[:, lanes], gm_pair.at[:, lanes], wg_ss.at[0], wgc_rs.at[2 * g + 1], sibling)
 
     def weight_to_z():
+        for g in range(2):
+            wait(x_pair.at[:, group_lanes(g)], wgc_rs.at[2 * g])
+            wait(gm_pair.at[:, group_lanes(g)], wgc_rs.at[2 * g + 1])
+
+        def term(zz):
+            total = 0
+            for left, right in ((xin, gm_buf), (x_pair, gm_pair)):
+                total = total + lax.dot_general(
+                    left[slab(zz, core), :], right[...], (((1,), (1,)), ((), ())), preferred_element_type=f32
+                )
+            return total
+
         def one(zz):
-            wait(wgc_recv.at[zz], wgc_rs.at[zz])
-            wgz_send[zz] = (wgp[slab(zz, core), :] + wgc_recv[zz]).astype(bf16)
+            wgz_send[zz] = term(zz).astype(bf16)
             send(wgz_send.at[zz], wgz_recv.at[z], wg_ss.at[1], wgz_rs.at[z], to(zz))
 
         others(one)
-        wait(wgc_recv.at[z], wgc_rs.at[z])
+        wg_half[...] = term(z)
 
     def weight_to_x():
-        wg_half[...] = wgp[slab(z, core), :] + wgc_recv[z]
-
         def one(zz):
             wait(wgz_recv.at[zz], wgz_rs.at[zz])
             wg_half[...] += wgz_recv[zz].astype(f32)
@@ -499,6 +500,7 @@
         own_wg.start()
 
     weight_start()
+    spread_cotangent()
     messages(0)
     wait(tab_in, tab_sems.at[2])
     sib_tab = pltpu.make_async_copy(tab_in, tab_sib, tab_sems.at[3])
@@ -506,12 +508,8 @@
     own_tab.wait()
     sib_tab.wait()
     pair_messages_in(0)
-    weight_forward(1)
     far(0)
-    weight_forward(2)
     close(0, False)
-    weight_forward(3)
-    spread_cotangent()
     messages(1)
     close(0, True)
     pair_messages_in(1)
@@ -520,21 +518,23 @@
     close(1, False)
     finish_sums(0)
     close(1, True)
+    weight_share()
     mix(0)
     second_axis_sums(1)
     gather_own(0)
     finish_sums(1)
+    give_act(0)
     gather_near(0)
+    weight_inputs(0)
     gather_far(0)
     mix(1)
+    weight_inputs(1)
     take(0, 0)
     take(0, 1)
-    weight_terms()
     take(0, 2)
+    weight_to_z()
     take(0, 3)
     gather_own(1)
-    weight_to_z()
-    give_act(0)
     give_act(1)
     fg_acc[...] = jnp.zeros_like(fg_acc)
     take_last(0)
@@ -544,16 +544,17 @@
     backward(0, 0, 3)
     take(1, 0)
     backward(0, 3, 6)
-    weight_to_x()
     take(1, 1)
     take(1, 2)
+    weight_to_x()
+    take(1, 3)
     weight_to_y()
-    take(1, 3)
+    take_last(1)
     weight_back_x()
-    take_last(1)
+    backward_ready(1)
+    backward(1, 0, 3)
     weight_done()
-    backward_ready(1)
-    backward(1, 0, BATCHES)
+    backward(1, 3, BATCHES)
     backward_done()
 
     own_wg.wait()
@@ -570,10 +571,11 @@
     wait(t1_send, t_ss.at[0])
     wait(t2_send, t_ss.at[1])
     seven = pl.ds(0, (FEAT - 1) * W)
-    wait(wfull.at[seven, :], z_ss.at[0])
+    for k in (0, 5):
+        wait(wfull.at[seven, half_cols], z_ss.at[k])
     for k in range(1, 5):
         wait(cot_in.at[seven, :], z_ss.at[k])
-    wait(wgc_recv, wg_ss.at[0])
+    wait(wfull.at[:, pl.ds(0, 2 * CHUNK)], wg_ss.at[0])
     wait(wgz_send.at[pl.ds(0, FEAT - 1)], wg_ss.at[1])
     for k in (2, 3, 4):
         wait(wx_send.at[pl.ds(0, SIDE - 1)], wg_ss.at[k])
@@ -610,7 +612,7 @@
             vmem((2 * LB, *block), bf16),
             vmem((D, CHUNK), bf16), vmem((D, D), bf16), vmem((D, CHUNK), bf16),
             vmem((D, CHUNK), bf16), vmem((D, CHUNK), bf16), vmem((D, CHUNK), bf16),
-            vmem((D, D), f32), vmem((FEAT, W // 2, D), f32),
+            vmem((D, CHUNK), bf16), vmem((D, CHUNK), bf16),
             vmem((FEAT, W // 2, D), bf16), vmem((FEAT, W // 2, D), bf16),
             vmem((SIDE, 9, 8, 128), f32), vmem((SIDE, 9, 8, 128), f32),
             vmem((9, 8, 128), f32), vmem((SIDE, 9, 8, 128), f32),
@@ -618,9 +620,9 @@
             vmem((W // 2, D), f32),
             dma((2 * BATCHES,)), dma((4,)), dma((2,)), dma((2 * BATCHES,)),
             dma, dma((32,)), dma, dma((64,)), dma((2,)), dma((8,)), dma((16,)),
-            dma((5,)), dma((2 * FEAT,)), dma((FEAT,)), dma((2 * FEAT,)), dma((2 * FEAT,)), dma((2 * FEAT,)), dma((5,)),
+            dma((6,)), dma((2 * FEAT,)), dma((2 * FEAT,)), dma((2 * FEAT,)), dma((2 * FEAT,)), dma((2 * FEAT,)), dma((5,)),
             dma((2,)), dma((16,)), dma((8,)), dma((64,)), dma((32,)), dma((2,)),
-            dma((6,)), dma((FEAT,)), dma((FEAT,)), dma((SIDE,)), dma((SIDE,)), dma((SIDE,)), dma,
+            dma((6,)), dma((4,)), dma((FEAT,)), dma((SIDE,)), dma((SIDE,)), dma((SIDE,)), dma,
         ],
         compiler_params=pltpu.CompilerParams(
             collective_id=0, has_side_effects=True, vmem_limit_bytes=VMEM_LIMIT

time: 122 us -> 114 us (0.934)
  Pallas kernels: 116 us -> 108 us
    pallas_call x1, Pallas kernels: 116 us -> 108 us  [exchange(): pl.pallas_call(exchange_kernel, in_specs=[smem_spec, smem_spec, vmem_spec...]
where the time goes in v4:
time: 114 us; the launch traced here: 113 us
  Pallas kernels  108 us (95%)
  local copies, waits for them, and re-layouts  5.23 us (5%)
    pallas_call x1, Pallas kernels, exchange(): pl.pallas_call(exchange_kernel, in_specs=[smem_spec, smem_spec, vmem_spec...  108 us
    unnamed x3, local copies, waits for them, and re-layouts  5.23 us

profile of v4, /device:TPU:1, one launch (start us, length us, event | category | flops | bytes accessed | tf_op | source)
XLA Modules:
  0.0 113.4 jit_solution(4178684368109616091)
XLA Ops:
  0.6 107.6 %shard_map.85 = (bf16[96,2048]{1,0:T(8,128)(2,1)}, f32[96,768]{1,0:T(8,128)}, bf16[96,2048]{1,0:T(8,128)(2,1)}) custom-call(s32[24]{0:T(128)} %doc_ref.1, s32[24]{0:T(128)} %label_ref.1, bf16[96,2048]{1,0:T(8,128)(2,1)} %bitcast.4, bf16[24,512,512]{2,1,0:T(8,128)(2,1)} %inc.1, bf16[96,768]{1,0:T(8,128)(2,1)} %weight.1, bf16[96,2048]{1,0:T(8,128)(2,1)} %bitcast.5), custom_call_target="tpu_custom_call" | custom-call | tf_op jit(solution)/shard_map/pallas_call | solution.py:593
  108.2 1.8 %copy.12 = bf16[2048,96]{0,1:T(8,128)(2,1)} copy(bf16[2048,96]{0,1:T(8,128)(2,1)} %bitcast.7) | data formatting | bytes 786432
  110.0 1.7 %copy.13 = f32[96,768]{1,0:T(8,128)} copy(f32[96,768]{1,0:T(8,128)} %get-tuple-element.13) | data formatting | bytes 589824
  111.7 1.8 %copy.14 = bf16[2048,96]{0,1:T(8,128)(2,1)} copy(bf16[2048,96]{0,1:T(8,128)(2,1)} %bitcast.6) | data formatting | bytes 786432

commit v5 on v4

--- a/solution.py
+++ b/solution.py
@@ -512,9 +512,9 @@
     close(0, False)
     messages(1)
     close(0, True)
+    second_axis_sums(0)
     pair_messages_in(1)
     far(1)
-    second_axis_sums(0)
     close(1, False)
     finish_sums(0)
     close(1, True)
@@ -630,9 +630,29 @@
     )(doc, label, feat, inc, weight, cot)
 
 
+def results_kernel(*refs):
+    half = len(refs) // 2
+    ins, outs, sems = refs[:half], refs[half : 2 * half], refs[-1]
+    copies = [pltpu.make_async_copy(i, o, sems.at[k]) for k, (i, o) in enumerate(zip(ins, outs))]
+    for copy in copies:
+        copy.start()
+    for copy in copies:
+        copy.wait()
+
+
+def results(*arrays):
+    return pl.pallas_call(
+        results_kernel,
+        in_specs=[pl.BlockSpec(memory_space=pl.ANY)] * len(arrays),
+        out_specs=[pl.BlockSpec(memory_space=pltpu.VMEM)] * len(arrays),
+        out_shape=[jax.ShapeDtypeStruct(a.shape, a.dtype) for a in arrays],
+        scratch_shapes=[pltpu.SemaphoreType.DMA((len(arrays),))],
+    )(*arrays)
+
+
 def local(features, pair_doc, pair_label, incidence, weight, cotangent):
-    act, weight_grad, feature_grad = exchange(
-        pair_doc, pair_label, features.T, incidence, weight, cotangent.T
+    act, weight_grad, feature_grad = results(
+        *exchange(pair_doc, pair_label, features.T, incidence, weight, cotangent.T)
     )
     return act.T, weight_grad, feature_grad.T
 

time: 114 us -> 107 us (0.939)
  local copies, waits for them, and re-layouts: 5.23 us -> 0 us
    unnamed x3 -> x0, local copies, waits for them, and re-layouts: 5.23 us -> none
    pallas_call x1, Pallas kernels: 108 us -> 104 us  [exchange(): pl.pallas_call(exchange_kernel, in_specs=[smem_spec, smem_spec, vmem_spec...]
    pallas_call x0 -> x1, Pallas kernels: none -> 2.2 us  [results(): pl.pallas_call(results_kernel, in_specs=[pl.BlockSpec(memory_space=pl.ANY...]
where the time goes in v5:
time: 107 us
  Pallas kernels  107 us (100%)
    pallas_call x1, Pallas kernels, exchange(): pl.pallas_call(exchange_kernel, in_specs=[smem_spec, smem_spec, vmem_spec...  104 us
    pallas_call x1, Pallas kernels, results(): pl.pallas_call(results_kernel, in_specs=[pl.BlockSpec(memory_space=pl.ANY...  2.2 us

profile of v5, /device:TPU:1, one launch (start us, length us, event | category | flops | bytes accessed | tf_op | source)
XLA Modules:
  0.0 107.3 jit_solution(591816228543682747)
XLA Ops:
  0.6 104.4 %shard_map.85 = (bf16[96,2048]{1,0:T(8,128)(2,1)}, f32[96,768]{1,0:T(8,128)}, bf16[96,2048]{1,0:T(8,128)(2,1)}) custom-call(s32[24]{0:T(128)} %doc_ref.1, s32[24]{0:T(128)} %label_ref.1, bf16[96,2048]{1,0:T(8,128)(2,1)} %bitcast.4, bf16[24,512,512]{2,1,0:T(8,128)(2,1)} %inc.1, bf16[96,768]{1,0:T(8,128)(2,1)} %weight.1, bf16[96,2048]{1,0:T(8,128)(2,1)} %bitcast.5), custom_call_target="tpu_custom_call" | custom-call | tf_op jit(solution)/shard_map/pallas_call | solution.py:593
  105.1 2.2 %shard_map.86 = (bf16[96,2048]{1,0:T(8,128)(2,1)}, f32[96,768]{1,0:T(8,128)}, bf16[96,2048]{1,0:T(8,128)(2,1)}) custom-call(bf16[96,2048]{1,0:T(8,128)(2,1)} %get-tuple-element.9.refs_0_, f32[96,768]{1,0:T(8,128)} %get-tuple-element.10.refs_1_, bf16[96,2048]{1,0:T(8,128)(2,1)} %get-tuple-element.11.refs_2_), custom_call_target="tpu_custom_call" | custom-call | tf_op jit(solution)/shard_map/pallas_call | solution.py:644

commit v6 on v5

--- a/solution.py
+++ b/solution.py
@@ -44,7 +44,7 @@
     tiles, inc_buf, msg_a, msg_b, tab, tab_out, tab_in, tab_own, tab_sib,
     s1_send, s1_recv, s2_send, s2_recv, t1_send, t1_recv, t2_send, t2_recv,
     summed, xin, wfull, cot_in, act_buf, gm_buf, gmt_buf,
-    x_pair, gm_pair, wgz_send, wgz_recv, wx_send, wx_recv, wy_send, wy_recv, wf_send, wf_recv, wg_half,
+    wflip, x_pair, gm_pair, wgz_send, wgz_recv, wx_send, wx_recv, wy_send, wy_recv, wf_send, wf_recv, wg_half,
     inc_sem, tab_sems, sib_ss, sib_rs, s1_ss, s1_rs, s2_ss, s2_rs, t_ss, t1_rs, t2_rs,
     z_ss, x_rs, w_rs, cot_rs, act_rs, gz_rs, local_sem,
     ag_ss, p1_rs, p2_rs, q1_rs, q2_rs, pair_rs,
@@ -289,15 +289,19 @@
     def mix(g):
         if g == 0:
             others(lambda zz: wait(wfull.at[rows_at(zz), other_cols], w_rs.at[FEAT + zz]))
+
+            def flip(o):
+                rows = pl.ds(pl.multiple_of(o * CHUNK, CHUNK), CHUNK)
+                wflip[rows, :] = wfull[:, rows].T
+
+            loop(D // CHUNK, flip)
             for gg in range(2):
                 others(lambda zz: wait(cot_in.at[rows_at(zz), group_lanes(gg)], cot_rs.at[gg * FEAT + zz]))
         others(lambda zz: wait(xin.at[rows_at(zz), group_lanes(g)], x_rs.at[g * FEAT + zz]))
 
         def forth(o):
             rows = pl.ds(pl.multiple_of(o * CHUNK, CHUNK), CHUNK)
-            mixed = lax.dot_general(
-                wfull[:, rows], xin[:, group_lanes(g)], (((0,), (0,)), ((), ())), preferred_element_type=f32
-            )
+            mixed = jnp.dot(wflip[rows, :], xin[:, group_lanes(g)], preferred_element_type=f32)
             gate = jax.nn.sigmoid(mixed)
             act_buf[rows, group_lanes(g)] = (mixed * gate).astype(bf16)
             slope = gate * (1.0 + mixed * (1.0 - gate))
@@ -436,20 +440,21 @@
             wait(x_pair.at[:, group_lanes(g)], wgc_rs.at[2 * g])
             wait(gm_pair.at[:, group_lanes(g)], wgc_rs.at[2 * g + 1])
 
-        def term(zz):
+        lefts = [
+            jnp.concatenate([left[slab(s, core), :] for s in range(FEAT)], axis=0) for left in (xin, x_pair)
+        ]
+        for n in range(D // CHUNK):
+            columns = slice(n * CHUNK, (n + 1) * CHUNK)
             total = 0
-            for left, right in ((xin, gm_buf), (x_pair, gm_pair)):
+            for left, right in zip(lefts, (gm_buf, gm_pair)):
                 total = total + lax.dot_general(
-                    left[slab(zz, core), :], right[...], (((1,), (1,)), ((), ())), preferred_element_type=f32
+                    left, right[columns, :], (((1,), (1,)), ((), ())), preferred_element_type=f32
                 )
-            return total
-
-        def one(zz):
-            wgz_send[zz] = term(zz).astype(bf16)
-            send(wgz_send.at[zz], wgz_recv.at[z], wg_ss.at[1], wgz_rs.at[z], to(zz))
-
-        others(one)
-        wg_half[...] = term(z)
+            for s in range(FEAT):
+                wgz_send[s, :, columns] = total[s * HALF : (s + 1) * HALF].astype(bf16)
+
+        others(lambda zz: send(wgz_send.at[zz], wgz_recv.at[z], wg_ss.at[1], wgz_rs.at[z], to(zz)))
+        wg_half[...] = wgz_send[z].astype(f32)
 
     def weight_to_x():
         def one(zz):
@@ -612,7 +617,7 @@
             vmem((2 * LB, *block), bf16),
             vmem((D, CHUNK), bf16), vmem((D, D), bf16), vmem((D, CHUNK), bf16),
             vmem((D, CHUNK), bf16), vmem((D, CHUNK), bf16), vmem((D, CHUNK), bf16),
-            vmem((D, CHUNK), bf16), vmem((D, CHUNK), bf16),
+            vmem((D, D), bf16), vmem((D, CHUNK), bf16), vmem((D, CHUNK), bf16),
             vmem((FEAT, W // 2, D), bf16), vmem((FEAT, W // 2, D), bf16),
             vmem((SIDE, 9, 8, 128), f32), vmem((SIDE, 9, 8, 128), f32),
             vmem((9, 8, 128), f32), vmem((SIDE, 9, 8, 128), f32),

time: 107 us -> 106 us (level)
  no operation moved by 1% of the time
where the time goes in v6:
time: 106 us
  Pallas kernels  106 us (100%)
    pallas_call x1, Pallas kernels, exchange(): pl.pallas_call(exchange_kernel, in_specs=[smem_spec, smem_spec, vmem_spec...  103 us
    pallas_call x1, Pallas kernels, results(): pl.pallas_call(results_kernel, in_specs=[pl.BlockSpec(memory_space=pl.ANY...  2.2 us

profile of v6, /device:TPU:1, one launch (start us, length us, event | category | flops | bytes accessed | tf_op | source)
XLA Modules:
  0.0 106.3 jit_solution(12076864342070926233)
XLA Ops:
  0.6 103.5 %shard_map.85 = (bf16[96,2048]{1,0:T(8,128)(2,1)}, f32[96,768]{1,0:T(8,128)}, bf16[96,2048]{1,0:T(8,128)(2,1)}) custom-call(s32[24]{0:T(128)} %doc_ref.1, s32[24]{0:T(128)} %label_ref.1, bf16[96,2048]{1,0:T(8,128)(2,1)} %bitcast.4, bf16[24,512,512]{2,1,0:T(8,128)(2,1)} %inc.1, bf16[96,768]{1,0:T(8,128)(2,1)} %weight.1, bf16[96,2048]{1,0:T(8,128)(2,1)} %bitcast.5), custom_call_target="tpu_custom_call" | custom-call | tf_op jit(solution)/shard_map/pallas_call | solution.py:598
  104.1 2.2 %shard_map.86 = (bf16[96,2048]{1,0:T(8,128)(2,1)}, f32[96,768]{1,0:T(8,128)}, bf16[96,2048]{1,0:T(8,128)(2,1)}) custom-call(bf16[96,2048]{1,0:T(8,128)(2,1)} %get-tuple-element.9.refs_0_, f32[96,768]{1,0:T(8,128)} %get-tuple-element.10.refs_1_, bf16[96,2048]{1,0:T(8,128)(2,1)} %get-tuple-element.11.refs_2_), custom_call_target="tpu_custom_call" | custom-call | tf_op jit(solution)/shard_map/pallas_call | solution.py:649

commit v7 on v6

--- a/solution.py
+++ b/solution.py
@@ -545,13 +545,14 @@
     take_last(0)
     gather_near(1)
     gather_far(1)
+    take(1, 0)
     backward_ready(0)
-    backward(0, 0, 3)
-    take(1, 0)
-    backward(0, 3, 6)
+    backward(0, 0, 2)
     take(1, 1)
+    backward(0, 2, 4)
     take(1, 2)
     weight_to_x()
+    backward(0, 4, 6)
     take(1, 3)
     weight_to_y()
     take_last(1)

time: 106 us -> 106 us (level); the launches traced: 106 us -> 105 us
    pallas_call x1, Pallas kernels: 103 us -> 102 us  [exchange(): pl.pallas_call(exchange_kernel, in_specs=[smem_spec, smem_spec, vmem_spec...]
where the time goes in v7:
time: 106 us; the launch traced here: 105 us
  Pallas kernels  105 us (99%)
    pallas_call x1, Pallas kernels, exchange(): pl.pallas_call(exchange_kernel, in_specs=[smem_spec, smem_spec, vmem_spec...  102 us
    pallas_call x1, Pallas kernels, results(): pl.pallas_call(results_kernel, in_specs=[pl.BlockSpec(memory_space=pl.ANY...  2.2 us

profile of v7, /device:TPU:1, one launch (start us, length us, event | category | flops | bytes accessed | tf_op | source)
XLA Modules:
  0.0 105.2 jit_solution(17436227598139767241)
XLA Ops:
  0.6 102.4 %shard_map.85 = (bf16[96,2048]{1,0:T(8,128)(2,1)}, f32[96,768]{1,0:T(8,128)}, bf16[96,2048]{1,0:T(8,128)(2,1)}) custom-call(s32[24]{0:T(128)} %doc_ref.1, s32[24]{0:T(128)} %label_ref.1, bf16[96,2048]{1,0:T(8,128)(2,1)} %bitcast.4, bf16[24,512,512]{2,1,0:T(8,128)(2,1)} %inc.1, bf16[96,768]{1,0:T(8,128)(2,1)} %weight.1, bf16[96,2048]{1,0:T(8,128)(2,1)} %bitcast.5), custom_call_target="tpu_custom_call" | custom-call | tf_op jit(solution)/shard_map/pallas_call | solution.py:599
  103.0 2.2 %shard_map.86 = (bf16[96,2048]{1,0:T(8,128)(2,1)}, f32[96,768]{1,0:T(8,128)}, bf16[96,2048]{1,0:T(8,128)(2,1)}) custom-call(bf16[96,2048]{1,0:T(8,128)(2,1)} %get-tuple-element.9.refs_0_, f32[96,768]{1,0:T(8,128)} %get-tuple-element.10.refs_1_, bf16[96,2048]{1,0:T(8,128)(2,1)} %get-tuple-element.11.refs_2_), custom_call_target="tpu_custom_call" | custom-call | tf_op jit(solution)/shard_map/pallas_call | solution.py:650
